TPU v7x, 256 devices: a whole 4x4x8 slice. The times are simulated.
256 devices in a mesh: frame: 8 (over y, core), row: 32 (over z, x).
Axes of the slice: x: 4, y: 4, z: 8, core: 2. Of those that a mesh axis runs over, the one named last changes fastest.
Arguments:
- latents: bfloat16 [16, 32, 106, 320], P('frame', 'row'), may hold values from -6 to 6
- segments: int32 [16], replicated, may hold values from 0 to 7, never falling along the last dimension, each value on 1 to 6 neighbouring positions
- w_spatial: bfloat16 [3, 3, 320, 320], replicated, may hold values from -0.109375 to 0.109375
- w_temporal: bfloat16 [3, 320, 320], replicated, may hold values from -0.1875 to 0.1875
- w_qkv: bfloat16 [320, 960], replicated, may hold values from -3 to 3, as said below
- w_out: bfloat16 [320, 320], replicated, may hold values from -0.3125 to 0.3125
- cotangent: bfloat16 [16, 32, 106, 320], P('frame', 'row'), may hold values from -6 to 6
Outputs:
- grad_input: bfloat16 [16, 32, 106, 320], P('frame', 'row')
- grad_w_spatial: float32 [3, 3, 320, 320], replicated
- grad_w_temporal: float32 [3, 320, 320], replicated
- grad_w_qkv: float32 [320, 960], replicated
- grad_w_out: float32 [320, 320], replicated
Inputs may be any that keep to these rules, and one draw needn't show every extreme that they name: `w_qkv`: projection weights between -3 and 3.
All inputs are finite; a program needn't handle non-finite values.
Results may differ from a plain program's by a relative error of at most 0.02.
Values may be sent and summed in bfloat16 or wider, within the bound.
A program may use at most 64 MiB of HBM per device.

v0:
```python
import math

import jax
import jax.numpy as jnp
from jax import lax
from jax.sharding import PartitionSpec as P

HEADS = 8


def extended(cells, sides, width):
    for axis, dim in sides:
        count = lax.axis_size(axis)
        ends = count - 1
        head = lax.slice_in_dim(cells, 0, width, axis=dim)
        tail = lax.slice_in_dim(cells, cells.shape[dim] - width, cells.shape[dim], axis=dim)
        cells = jnp.concatenate(
            [
                lax.ppermute(tail, axis, [(i, (i + 1) % count) for i in range(ends)]),
                cells,
                lax.ppermute(head, axis, [((i + 1) % count, i) for i in range(ends)]),
            ],
            axis=dim,
        )
    return cells


def silu_grad(values):
    sig = jax.nn.sigmoid(values)
    return sig * (1.0 + values * (1.0 - sig))


def project(inputs, weights):
    flat = inputs.reshape(-1, inputs.shape[-1])
    result = jnp.dot(flat, weights, preferred_element_type=jnp.float32)
    return result.reshape(inputs.shape[:-1] + (weights.shape[-1],))


def conv_taps(padded, weights, row_count, col_count):
    summed = jnp.zeros(padded.shape[:1] + (row_count, col_count, weights.shape[-1]), jnp.float32)
    for tap_row in range(3):
        for tap_col in range(3):
            window = padded[:, tap_row : tap_row + row_count, tap_col : tap_col + col_count, :]
            summed = summed + project(window, weights[tap_row, tap_col])
    return summed


def conv_back(d_padded, weights, row_count, col_count):
    summed = jnp.zeros(d_padded.shape[:1] + (row_count, col_count, weights.shape[-2]), jnp.float32)
    for tap_row in range(3):
        for tap_col in range(3):
            window = d_padded[
                :, 2 - tap_row : 2 - tap_row + row_count, 2 - tap_col : 2 - tap_col + col_count, :
            ]
            summed = summed + project(window, weights[tap_row, tap_col].T)
    return summed


def spatial_grad(padded, d_out, row_count, col_count):
    channels = padded.shape[-1]
    flat_d = d_out.reshape(-1, d_out.shape[-1])
    taps = []
    for tap_row in range(3):
        for tap_col in range(3):
            window = padded[
                :, tap_row : tap_row + row_count, tap_col : tap_col + col_count, :
            ].reshape(-1, channels)
            taps.append(jnp.dot(window.T, flat_d, preferred_element_type=jnp.float32))
    return jnp.stack(taps).reshape(3, 3, channels, flat_d.shape[-1])


def pair_product(form, left, right):
    return jnp.einsum(form, left, right, preferred_element_type=jnp.float32)


def temporal_block(spatial, cotangent, segments, w_temporal, w_qkv, w_out):
    frames, pixels, channels = spatial.shape
    head_count = HEADS
    head_dim = channels // head_count
    score_scale = 1.0 / head_dim**0.5
    same_shot = segments[:, None] == segments[None, :]
    next_ok = jnp.concatenate(
        [(segments[1:] == segments[:-1]).astype(jnp.float32), jnp.zeros((1,), jnp.float32)]
    )
    prev_ok = jnp.concatenate([jnp.zeros((1,), jnp.float32), next_ok[:-1]])
    spatial_f = spatial.astype(jnp.float32)
    act_mid = jax.nn.silu(spatial_f).astype(jnp.bfloat16)
    zero_frame = jnp.zeros((1, pixels, channels), jnp.bfloat16)
    prev_t = (
        jnp.concatenate([zero_frame, act_mid[:-1]]) * prev_ok.astype(jnp.bfloat16)[:, None, None]
    )
    next_t = (
        jnp.concatenate([act_mid[1:], zero_frame]) * next_ok.astype(jnp.bfloat16)[:, None, None]
    )
    temporal = (
        spatial_f
        + project(prev_t, w_temporal[0])
        + project(act_mid, w_temporal[1])
        + project(next_t, w_temporal[2])
    ).astype(jnp.bfloat16)
    temporal_f = temporal.astype(jnp.float32)
    centred = temporal_f - jnp.mean(temporal_f, axis=-1, keepdims=True)
    inv_std = lax.rsqrt(jnp.mean(centred * centred, axis=-1, keepdims=True) + 1e-05)
    nhat = centred * inv_std
    normed = nhat.astype(jnp.bfloat16)
    qkv_all = project(normed, w_qkv)
    split_shape = (frames, pixels, head_count, head_dim)
    queries = qkv_all[..., :channels].astype(jnp.bfloat16).reshape(split_shape)
    key_vecs = qkv_all[..., channels : 2 * channels].astype(jnp.bfloat16).reshape(split_shape)
    values = qkv_all[..., 2 * channels :].astype(jnp.bfloat16).reshape(split_shape)
    scores = pair_product("fphd,gphd->phfg", queries, key_vecs) * score_scale
    scores = jnp.where(same_shot[None, None], scores, -1e30)
    row_peak = jnp.max(scores, axis=-1, keepdims=True)
    expo = jnp.exp(scores - row_peak)
    attn_prob = expo / jnp.sum(expo, axis=-1, keepdims=True)
    prob_b = attn_prob.astype(jnp.bfloat16)
    mixed = (
        pair_product("phfg,gphd->fphd", prob_b, values)
        .astype(jnp.bfloat16)
        .reshape(frames, pixels, channels)
    )
    flat_cot = cotangent.reshape(-1, channels)
    grad_out = jnp.dot(mixed.reshape(-1, channels).T, flat_cot, preferred_element_type=jnp.float32)
    d_mixed = project(cotangent, w_out.T).astype(jnp.bfloat16).reshape(split_shape)
    d_prob = pair_product("fphd,gphd->phfg", d_mixed, values)
    d_value = pair_product("phfg,fphd->gphd", prob_b, d_mixed).astype(jnp.bfloat16)
    d_score = (
        attn_prob * (d_prob - jnp.sum(attn_prob * d_prob, axis=-1, keepdims=True)) * score_scale
    ).astype(jnp.bfloat16)
    d_query = pair_product("phfg,gphd->fphd", d_score, key_vecs).astype(jnp.bfloat16)
    d_key = pair_product("phfg,fphd->gphd", d_score, queries).astype(jnp.bfloat16)
    d_qkv = jnp.concatenate(
        [
            d_query.reshape(frames, pixels, channels),
            d_key.reshape(frames, pixels, channels),
            d_value.reshape(frames, pixels, channels),
        ],
        axis=-1,
    )
    grad_qkv = jnp.dot(
        normed.reshape(-1, channels).T,
        d_qkv.reshape(-1, 3 * channels),
        preferred_element_type=jnp.float32,
    )
    d_normed = project(d_qkv, w_qkv.T)
    ln_back = inv_std * (
        d_normed
        - jnp.mean(d_normed, axis=-1, keepdims=True)
        - nhat * jnp.mean(d_normed * nhat, axis=-1, keepdims=True)
    )
    d_temporal = (cotangent.astype(jnp.float32) + ln_back).astype(jnp.bfloat16)
    flat_dt = d_temporal.reshape(-1, channels)
    grad_time = jnp.stack(
        [
            jnp.dot(prev_t.reshape(-1, channels).T, flat_dt, preferred_element_type=jnp.float32),
            jnp.dot(act_mid.reshape(-1, channels).T, flat_dt, preferred_element_type=jnp.float32),
            jnp.dot(next_t.reshape(-1, channels).T, flat_dt, preferred_element_type=jnp.float32),
        ]
    )
    back_prev = project(d_temporal, w_temporal[0].T)
    back_mid = project(d_temporal, w_temporal[1].T)
    back_next = project(d_temporal, w_temporal[2].T)
    zero_f = jnp.zeros((1, pixels, channels), jnp.float32)
    carried = (
        back_mid
        + jnp.concatenate([back_prev[1:], zero_f]) * next_ok[:, None, None]
        + jnp.concatenate([zero_f, back_next[:-1]]) * prev_ok[:, None, None]
    )
    d_spatial = (d_temporal.astype(jnp.float32) + silu_grad(spatial_f) * carried).astype(
        jnp.bfloat16
    )
    return (d_spatial, (grad_time, grad_qkv, grad_out))


def pad_columns(block):
    return jnp.pad(block, ((0, 0), (0, 0), (1, 1), (0, 0)))


def on_device(latents, segments, w_spatial, w_temporal, w_qkv, w_out, cotangent):
    frames_dev, row_count, col_count, channels = latents.shape
    groups = lax.axis_size("frame")
    latent_wide = latents.astype(jnp.float32)
    act_in = jax.nn.silu(latent_wide).astype(jnp.bfloat16)
    act_pad = pad_columns(extended(act_in, (("row", 1),), 1))
    spatial = (latent_wide + conv_taps(act_pad, w_spatial, row_count, col_count)).astype(
        jnp.bfloat16
    )
    pixels = row_count * col_count
    slot_count = -(-pixels // groups)
    padded_width = slot_count * groups

    def to_slots(block):
        flat = block.reshape(frames_dev, pixels, channels)
        return jnp.pad(flat, ((0, 0), (0, padded_width - pixels), (0, 0)))

    spatial_pix, cot_pix = (
        lax.all_to_all(to_slots(spatial), "frame", split_axis=1, concat_axis=0, tiled=True),
        lax.all_to_all(to_slots(cotangent), "frame", split_axis=1, concat_axis=0, tiled=True),
    )
    d_pix, grads_time = temporal_block(spatial_pix, cot_pix, segments, w_temporal, w_qkv, w_out)
    grad_time, grad_qkv, grad_out = grads_time
    d_frames = lax.all_to_all(d_pix, "frame", split_axis=0, concat_axis=1, tiled=True)
    d_spatial = d_frames[:, :pixels].reshape(frames_dev, row_count, col_count, channels)
    d_pad = pad_columns(extended(d_spatial, (("row", 1),), 1))
    grad_space = spatial_grad(act_pad, d_spatial, row_count, col_count)
    d_act = conv_back(d_pad, w_spatial, row_count, col_count)
    grad_input = (d_spatial.astype(jnp.float32) + silu_grad(latent_wide) * d_act).astype(
        jnp.bfloat16
    )
    grad_space, grad_time, grad_qkv, grad_out = lax.psum(
        (grad_space, grad_time, grad_qkv, grad_out), ("frame", "row")
    )
    positions = frames_dev * groups * row_count * lax.axis_size("row") * col_count
    factor = 1.0 / math.sqrt(positions)
    return (
        grad_input,
        grad_space * factor,
        grad_time * factor,
        grad_qkv * factor,
        grad_out * factor,
    )


def solution(mesh):
    in_specs = (
        P("frame", "row", None, None),
        P(),
        P(),
        P(),
        P(),
        P(),
        P("frame", "row", None, None),
    )
    out_specs = (P("frame", "row", None, None), P(), P(), P(), P())
    return jax.shard_map(
        on_device, mesh=mesh, in_specs=in_specs, out_specs=out_specs, check_vma=False
    )
```

profile of v0, /device:TPU:1, one launch (start us, length us, event | category | flops | bytes accessed | tf_op | source)
XLA Modules:
  0.0 455.5 jit_solution(14298404655695405088)
XLA Ops:
  10.6 5.2 %collective-permute-start = (bf16[2,1,106,320]{2,3,0,1:T(8,128)(2,1)S(1)}, bf16[2,1,106,320]{2,3,0,1:T(8,128)(2,1)}, u32[]{:S(2)}, u32[]{:S(2)}) collective-permute-start(bf16[2,1,106,320]{2,3,0,1:T(8,128)(2,1)S(1)} %fusion.61), channel_id=1, source_target_pairs={{0,1},{1,2},{2,3},{3,4},{4,5},{5,6},{6,7},{7,8},{8,9},{9,10},{10,1... | collective-permute-start | bytes 407048 | tf_op jit(solution)/shard_map/ppermute | solution.py:19
  17.6 6.5 %all-to-all-start = ((bf16[2,112,320]{2,0,1:T(2,128)(2,1)}), bf16[2,112,320]{2,0,1:T(2,128)(2,1)S(1)}, u32[]{:S(2)}, u32[]{:S(2)}) async-start(bf16[2,112,320]{2,0,1:T(2,128)(2,1)} %pad.18), calls=%async_computation | async-start | bytes 344064 | tf_op jit(solution)/shard_map/all_to_all | solution.py:198
  32.1 1.9 convolution_convert_fusion.5
  34.0 2.1 reshape.320
  46.2 4.8 %all-to-all-start.1 = ((bf16[2,112,320]{2,0,1:T(2,128)(2,1)}), bf16[2,112,320]{2,0,1:T(2,128)(2,1)}, u32[]{:S(2)}, u32[]{:S(2)}) async-start(bf16[2,112,320]{2,0,1:T(2,128)(2,1)} %pad.20.clone), calls=%async_computation.1 | async-start | bytes 344064 | tf_op jit(solution)/shard_map/all_to_all | solution.py:197
  66.3 1.8 convert.12
  81.8 2.1 reshape.321
  83.9 2.1 reshape.319
  86.0 2.1 reshape.318
  92.3 3.4 fusion.19
  95.8 3.6 fusion.18
  99.3 2.8 fusion.20
  102.1 2.9 fusion.21
  105.0 1.9 copy.293
  106.9 2.1 concatenate.48
  109.0 1.9 copy.295
  110.9 2.0 concatenate.49
  112.9 1.9 copy.297
  114.8 2.1 concatenate.50
  123.8 2.0 fusion.89
  125.8 2.0 fusion.94
  127.7 2.9 convolution_bitcast_fusion
  131.6 2.1 reshape_reshape.7
  133.6 1.8 slice.172
  135.4 1.8 copy.302
  142.3 4.8 %all-to-all-start.2 = ((bf16[16,14,320]{2,1,0:T(8,128)(2,1)}), bf16[16,14,320]{2,1,0:T(8,128)(2,1)S(1)}, u32[]{:S(2)}, u32[]{:S(2)}) async-start(bf16[16,14,320]{2,1,0:T(8,128)(2,1)} %copy.303), calls=%async_computation.2 | async-start | bytes 393216 | tf_op jit(solution)/shard_map/all_to_all | solution.py:202
  147.2 2.1 fusion.167
  149.2 2.5 pad_maximum_fusion
  159.2 2.1 copy-done.2
  162.8 4.0 collective-permute-start.2
  172.7 267.8 %all-reduce.11.cloned.1.call-done = (f32[3,3,320,320]{3,2,1,0:T(8,128)}, f32[3,320,320]{2,1,0:T(8,128)}, f32[320,960]{1,0:T(8,128)}, f32[320,320]{1,0:T(8,128)}) async-done(((f32[3,3,320,320]{3,2,1,0:T(8,128)}, f32[3,320,320]{2,1,0:T(8,128)}, f32[320,960]{1,0:T(8,128)}, f32[320,320]{1,0:T(8,128)}), (f32[3,3,320,320]{3,2,1,0:T(8,128)}, f32[3,320,320]{2,1,0:T(8,128)}, f32[320,960]{1,0:T(8,128)}, ...) | async-done | bytes 6553616 | tf_op jit(solution)/shard_map/psum | solution.py:210
  440.5 4.9 %broadcast_multiply_fusion = f32[3,3,320,320]{3,2,1,0:T(8,128)} fusion(f32[3,3,320,320]{3,2,1,0:T(8,128)} %get-tuple-element.37), kind=kLoop, calls=%fused_computation.2 | loop fusion | flops 921600 | bytes 7372800 | tf_op jit(solution)/shard_map/mul | solution.py:217
  (188 shorter events, 87.0 us)
Async XLA Ops:
  7.2 73.4 %copy-start = (bf16[320,960]{1,0:T(8,128)(2,1)S(1)}, bf16[320,960]{1,0:T(8,128)(2,1)}, u32[]{:S(2)}) copy-start(bf16[320,960]{1,0:T(8,128)(2,1)} %param.11) | copy-start | bytes 1843204
  9.1 27.0 %copy-start.12 = (bf16[2,1,106,320]{2,3,0,1:T(8,128)(2,1)}, bf16[2,1,106,320]{2,3,0,1:T(8,128)(2,1)S(1)}, u32[]{:S(2)}) copy-start(bf16[2,1,106,320]{2,3,0,1:T(8,128)(2,1)S(1)} %fusion.61) | copy-start | bytes 407044
  9.1 29.0 %copy-start.1 = (bf16[3,3,320,320]{3,2,1,0:T(8,128)(2,1)S(1)}, bf16[3,3,320,320]{3,2,1,0:T(8,128)(2,1)}, u32[]{:S(2)}) copy-start(bf16[3,3,320,320]{3,2,1,0:T(8,128)(2,1)} %param.9) | copy-start | bytes 5529604
  9.2 26.9 %collective-permute-start.1 = (bf16[2,1,106,320]{2,3,0,1:T(8,128)(2,1)S(1)}, bf16[2,1,106,320]{2,3,0,1:T(8,128)(2,1)S(1)}, u32[]{:S(2)}, u32[]{:S(2)}) collective-permute-start(bf16[2,1,106,320]{2,3,0,1:T(8,128)(2,1)S(1)} %fusion.61), channel_id=1, source_target_pairs={{1,0},{2,1},{3,2},{4,3},{5,4},{6,5},{7,6},{8,7},{9,8},{10,9},{11,1... | collective-permute-start | bytes 407048 | tf_op jit(solution)/shard_map/ppermute | solution.py:21
  10.6 26.2 %collective-permute-start = (bf16[2,1,106,320]{2,3,0,1:T(8,128)(2,1)S(1)}, bf16[2,1,106,320]{2,3,0,1:T(8,128)(2,1)}, u32[]{:S(2)}, u32[]{:S(2)}) collective-permute-start(bf16[2,1,106,320]{2,3,0,1:T(8,128)(2,1)S(1)} %fusion.61), channel_id=1, source_target_pairs={{0,1},{1,2},{2,3},{3,4},{4,5},{5,6},{6,7},{7,8},{8,9},{9,10},{10,1... | collective-permute-start | bytes 407048 | tf_op jit(solution)/shard_map/ppermute | solution.py:19
  17.6 12.2 %all-to-all-start = ((bf16[2,112,320]{2,0,1:T(2,128)(2,1)}), bf16[2,112,320]{2,0,1:T(2,128)(2,1)S(1)}, u32[]{:S(2)}, u32[]{:S(2)}) async-start(bf16[2,112,320]{2,0,1:T(2,128)(2,1)} %pad.18), calls=%async_computation | async-start | bytes 344064 | tf_op jit(solution)/shard_map/all_to_all | solution.py:198
  46.2 19.2 %all-to-all-start.1 = ((bf16[2,112,320]{2,0,1:T(2,128)(2,1)}), bf16[2,112,320]{2,0,1:T(2,128)(2,1)}, u32[]{:S(2)}, u32[]{:S(2)}) async-start(bf16[2,112,320]{2,0,1:T(2,128)(2,1)} %pad.20.clone), calls=%async_computation.1 | async-start | bytes 344064 | tf_op jit(solution)/shard_map/all_to_all | solution.py:197
  52.1 11.4 %copy-start.31 = (bf16[2,1,106,320]{2,3,0,1:T(8,128)(2,1)S(1)}, bf16[2,1,106,320]{2,3,0,1:T(8,128)(2,1)}, u32[]{:S(2)}) copy-start(bf16[2,1,106,320]{2,3,0,1:T(8,128)(2,1)} %get-tuple-element.45) | copy-start | bytes 407044
  53.2 11.2 %copy-start.30 = (bf16[2,1,106,320]{2,3,0,1:T(8,128)(2,1)S(1)}, bf16[2,1,106,320]{2,3,0,1:T(8,128)(2,1)}, u32[]{:S(2)}) copy-start(bf16[2,1,106,320]{2,3,0,1:T(8,128)(2,1)} %get-tuple-element.46) | copy-start | bytes 407044
  66.3 10.0 %copy-start.35 = (bf16[16]{0:T(256)(128)(2,1)S(1)}, bf16[16]{0:T(256)(128)(2,1)}, u32[]{:S(2)}) copy-start(bf16[16]{0:T(256)(128)(2,1)} %get-tuple-element.57) | copy-start | bytes 100
  70.2 8.7 %copy-start.3 = (f32[16,14,320]{2,0,1:T(8,128)}, f32[16,14,320]{2,0,1:T(8,128)S(1)}, u32[]{:S(2)}) copy-start(f32[16,14,320]{2,0,1:T(8,128)S(1)} %reshape.334) | copy-start | bytes 860164
  70.2 8.7 %copy-start.34 = (bf16[16]{0:T(256)(128)(2,1)S(1)}, bf16[16]{0:T(256)(128)(2,1)}, u32[]{:S(2)}) copy-start(bf16[16]{0:T(256)(128)(2,1)} %get-tuple-element.56) | copy-start | bytes 100
  75.7 5.3 %copy-start.18 = (bf16[15,14,320]{2,0,1:T(8,128)(2,1)}, bf16[15,14,320]{2,0,1:T(8,128)(2,1)S(1)}, u32[]{:S(2)}) copy-start(bf16[15,14,320]{2,0,1:T(8,128)(2,1)S(1)} %get-tuple-element.52) | copy-start | bytes 403204
  80.5 7.6 %copy-start.36 = (pred[16,16]{0,1:T(8,128)(4,1)S(1)}, pred[16,16]{0,1:T(8,128)(4,1)}, u32[]{:S(2)}) copy-start(pred[16,16]{0,1:T(8,128)(4,1)} %broadcast_compare_fusion) | copy-start | bytes 772
  88.1 2.9 copy-start.5
  88.1 2.9 copy-start.6
  118.8 3.0 copy-start.22
  127.7 2.9 copy-start.33
  130.7 9.4 %copy-start.4 = (f32[16,14,320]{2,0,1:T(8,128)S(1)}, f32[16,14,320]{2,0,1:T(8,128)}, u32[]{:S(2)}) copy-start(f32[16,14,320]{2,0,1:T(8,128)} %copy-done.3) | copy-start | bytes 860164
  130.7 9.4 %copy-start.23 = (bf16[16,14,320]{2,0,1:T(8,128)(2,1)S(1)}, bf16[16,14,320]{2,0,1:T(8,128)(2,1)}, u32[]{:S(2)}) copy-start(bf16[16,14,320]{2,0,1:T(8,128)(2,1)} %copy-done.22) | copy-start | bytes 430084
  130.7 9.4 %copy-start.37 = (f32[16]{0:T(128)S(1)}, f32[16]{0:T(128)}, u32[]{:S(2)}) copy-start(f32[16]{0:T(128)} %get-tuple-element.54) | copy-start | bytes 196
  130.7 9.4 %copy-start.38 = (f32[16]{0:T(128)S(1)}, f32[16]{0:T(128)}, u32[]{:S(2)}) copy-start(f32[16]{0:T(128)} %get-tuple-element.55) | copy-start | bytes 196
  142.3 10.7 %all-to-all-start.2 = ((bf16[16,14,320]{2,1,0:T(8,128)(2,1)}), bf16[16,14,320]{2,1,0:T(8,128)(2,1)S(1)}, u32[]{:S(2)}, u32[]{:S(2)}) async-start(bf16[16,14,320]{2,1,0:T(8,128)(2,1)} %copy.303), calls=%async_computation.2 | async-start | bytes 393216 | tf_op jit(solution)/shard_map/all_to_all | solution.py:202
  147.2 293.3 %all-reduce.11.cloned.1.call-start = ((), (), s32[]{:S(2)}) async-start(), calls=%async_computation.3 | async-start | bytes 15400960 | tf_op jit(solution)/shard_map/psum | solution.py:210
  153.2 4.6 %copy-start.24 = (bf16[212,320]{0,1:T(8,128)(2,1)S(1)}, bf16[212,320]{0,1:T(8,128)(2,1)}, u32[]{:S(2)}) copy-start(bf16[212,320]{0,1:T(8,128)(2,1)} %reshape.327) | copy-start | bytes 407044
  153.7 3.8 copy-start.29
  153.7 4.3 copy-start.28
  155.0 3.4 copy-start.27
  161.5 6.6 %collective-permute-start.3 = (bf16[2,1,106,320]{2,3,0,1:T(8,128)(2,1)S(1)}, bf16[2,1,106,320]{2,3,0,1:T(8,128)(2,1)S(1)}, u32[]{:S(2)}, u32[]{:S(2)}) collective-permute-start(bf16[2,1,106,320]{2,3,0,1:T(8,128)(2,1)S(1)} %bitcast.345), channel_id=1, source_target_pairs={{1,0},{2,1},{3,2},{4,3},{5,4},{6,5},{7,6},{8,7},{9,8},{10,9},{11,1... | collective-permute-start | bytes 407048 | tf_op jit(solution)/shard_map/ppermute | solution.py:21
  162.8 6.2 %collective-permute-start.2 = (bf16[2,1,106,320]{2,3,0,1:T(8,128)(2,1)S(1)}, bf16[2,1,106,320]{2,3,0,1:T(8,128)(2,1)S(1)}, u32[]{:S(2)}, u32[]{:S(2)}) collective-permute-start(bf16[2,1,106,320]{2,3,0,1:T(8,128)(2,1)S(1)} %bitcast.346), channel_id=1, source_target_pairs={{0,1},{1,2},{2,3},{3,4},{4,5},{5,6},{6,7},{7,8},{8,9},{9,10},{10,1... | collective-permute-start | bytes 407048 | tf_op jit(solution)/shard_map/ppermute | solution.py:19
  440.5 4.9 %copy-start.32 = (f32[320,320]{1,0:T(8,128)S(1)}, f32[320,320]{1,0:T(8,128)}, u32[]{:S(2)}) copy-start(f32[320,320]{1,0:T(8,128)} %get-tuple-element.40) | copy-start | bytes 1228804
  440.5 5.7 %copy-start.15 = (f32[320,960]{1,0:T(8,128)S(1)}, f32[320,960]{1,0:T(8,128)}, u32[]{:S(2)}) copy-start(f32[320,960]{1,0:T(8,128)} %get-tuple-element.39) | copy-start | bytes 3686404
  (15 other events, 23.9 us)
Sparse Core Ops, SparseCore 0:
  161.4 279.0 all-reduce.10
where the time goes:
time: 458 us; the launch traced here: 456 us
  waiting for transfers between devices  273 us (60%)
  local copies, waits for them, and re-layouts  69.5 us (15%)
  matrix products  49.5 us (11%)
  starting transfers between devices  28.1 us (6%)
  other arithmetic  21.1 us (5%)
  between operations  14.8 us (3%)
    psum x1, waiting for transfers between devices, on_device(): lax.psum((grad_space, grad_time, grad_qkv, grad_out), ('frame', 'row'))  268 us
    dot_general x25, matrix products, project(): result = jnp.dot(flat, weights, preferred_element_type=jnp.float32)  16.3 us
    dot_general x6, matrix products, pair_product(): return jnp.einsum(form, left, right, preferred_element_type=jnp.float32)  15.6 us
    ppermute x2, starting transfers between devices, extended(): lax.ppermute(tail, axis, [(i, (i + 1) % count) for i in range(ends)])  9.24 us
  transfers between devices with their start and end apart: 8, of which 5 were waited for; matrix products, arithmetic and copies ran while one was open for 8% of the time, Pallas kernels for 0%

commit v1 on v0

v1 whole, which is shorter than its diff:
```python
import math

import jax
import jax.numpy as jnp
from jax import lax
from jax.experimental import pallas as pl
from jax.experimental.pallas import tpu as pltpu
from jax.sharding import PartitionSpec as P

MESH = pl.DeviceIdType.MESH
BF = jnp.bfloat16
F32 = jnp.float32
HEADS = 8
C = 320
CP = 384
W = 106
WP = 112
ROWS = 2 * WP
UNIT = 128
GR = 1024
GL = 1024
NX, NY, NZ = 4, 4, 8


def nn(a, b):
    return lax.dot_general(a, b, (((1,), (0,)), ((), ())), preferred_element_type=F32)


def nt(a, b):
    return lax.dot_general(a, b, (((1,), (1,)), ((), ())), preferred_element_type=F32)


def tn(a, b):
    return lax.dot_general(a, b, (((0,), (0,)), ((), ())), preferred_element_type=F32)


def widen(x):
    return jnp.concatenate([x, jnp.zeros((x.shape[0], CP - C), x.dtype)], axis=1)


def pack3(a, b, c):
    b = pltpu.roll(b, 64, 1)
    return jnp.concatenate([a[:, :256], a[:, 256:] + b[:, :128], b[:, 128:], c], axis=1)


def silu_grad(v):
    sig = jax.nn.sigmoid(v)
    return sig * (1.0 + v * (1.0 - sig))


def up8(x):
    return jnp.concatenate([x[8:], jnp.zeros((8, x.shape[1]), x.dtype)], axis=0)


def down8(x):
    return jnp.concatenate([jnp.zeros((8, x.shape[1]), x.dtype), x[:-8]], axis=0)


def mega(
    seg, lat, cot, wsp_h, wt_h, wqkv_h, wout_h,
    gin, ft_out, fs_out,
    wsp, wt, wqkv, wq, wout, wo,
    latp, act, zbuf, snd_s, snd_c, rcv_s, rcv_c,
    u_act, u_dt, u_nrm, u_dq, u_mix, u_cot, snd_d, rcv_d,
    dp, dbuf, g_t, g_s, r0, r1, r2, r3, f_t, f_s, p1, p2, p3,
    wsem, hs, hr, a_s, a_r, dhs, dhr, s0s, s0r, s1s, s1r, s2s, s2r, s3s, s3r, osem,
):
    fr, row = lax.axis_index("frame"), lax.axis_index("row")
    y, core = fr // 2, fr % 2
    z, x = row // NX, row % NX
    nrow = NX * NZ

    def at(yy, cc, zz, xx):
        return {"frame": yy * 2 + cc, "row": zz * NX + xx}

    loads = [
        pltpu.make_async_copy(s, d, wsem.at[i])
        for i, (s, d) in enumerate([(wsp_h, wsp), (wt_h, wt), (wqkv_h, wqkv), (wout_h, wout)])
    ]
    for cp in loads:
        cp.start()

    def frame_peer(k):
        return {"frame": lax.rem(fr + k, 8), "row": row}

    def row_peer(k):
        return {"frame": fr, "row": lax.rem(row + k + nrow, nrow)}

    i1 = jnp.where(core == 0, x, y)
    i2 = jnp.where(core == 0, y, x)

    def first_peer(k):
        j = lax.rem(i1 + k, 4)
        return j, at(jnp.where(core == 0, y, j), core, z, jnp.where(core == 0, j, x))

    def second_peer(k):
        j = lax.rem(i2 + k, 4)
        return j, at(jnp.where(core == 0, j, y), core, z, jnp.where(core == 0, x, j))

    def z_peer(k):
        j = lax.rem(z + k, NZ)
        return j, at(y, core, j, x)

    sibling = at(y, 1 - core, z, x)

    barrier = pltpu.get_barrier_semaphore()
    peers = [frame_peer(k) for k in range(1, 8)]
    peers += [row_peer(1), row_peer(-1)]
    peers += [at(y, core, z, lax.rem(x + k, NX)) for k in range(1, NX)]
    peers += [z_peer(k)[1] for k in range(1, NZ)]
    for peer in peers:
        pl.semaphore_signal(barrier, inc=1, device_id=peer, device_id_type=MESH)

    def send(src, dst, ssem, rsem, peer):
        cp = pltpu.make_async_remote_copy(
            src_ref=src, dst_ref=dst, send_sem=ssem, recv_sem=rsem,
            device_id=peer, device_id_type=MESH,
        )
        cp.start()
        return cp

    latp[...] = jnp.zeros_like(latp)
    dp[...] = jnp.zeros_like(dp)
    for f in range(2):
        latp[f * WP : f * WP + W, :] = lat[f, 0].astype(F32)
        dp[f * WP : f * WP + W, :] = cot[f, 0].astype(F32)
    lv = latp[...]
    act[1] = (lv * jax.nn.sigmoid(lv)).astype(BF)

    def to_groups(src, dst):
        for g in range(16):
            if g < 14:
                t = jnp.concatenate(
                    [src[8 * g : 8 * g + 8, :], src[WP + 8 * g : WP + 8 * g + 8, :]], axis=0
                )
            else:
                t = jnp.zeros((16, C), F32)
            dst[g // 2, g % 2] = t.astype(BF)

    pl.semaphore_wait(barrier, len(peers))

    halo = [
        send(act.at[1], act.at[0], hs.at[0], hr.at[0], row_peer(1)),
        send(act.at[1], act.at[2], hs.at[1], hr.at[1], row_peer(-1)),
    ]

    def exchange(snd, rcv, ssem, rsem, base):
        cps = []
        for k in range(1, 8):
            cps.append(
                send(snd.at[lax.rem(fr + k, 8)], rcv.at[fr],
                     ssem.at[base + k - 1], rsem.at[base + k - 1], frame_peer(k))
            )
        rcv[pl.ds(fr, 1)] = snd[pl.ds(fr, 1)]
        return cps

    to_groups(dp, snd_c)
    cot_cps = exchange(snd_c, rcv_c, a_s, a_r, 0)

    for cp in loads:
        cp.wait()
    wo[...] = jnp.zeros_like(wo)
    wo[:C, :] = wout[...]
    for i in range(3):
        if i == 1:
            t = pltpu.roll(wqkv[:, 256:640].astype(F32), CP - 64, 1).astype(BF)
        else:
            t = wqkv[:, 640 * (i // 2) : 640 * (i // 2) + C]
        wq[i] = widen(t[:, :C])

    for cp in halo:
        cp.wait_recv()

    @pl.when(row == 0)
    def _():
        act[0] = jnp.zeros((ROWS, C), BF)

    @pl.when(row == nrow - 1)
    def _():
        act[2] = jnp.zeros((ROWS, C), BF)

    def conv_tap(b, carry):
        zbuf[b] = nn(act[0], wsp[0, b]) + nn(act[1], wsp[1, b]) + nn(act[2], wsp[2, b])
        return carry

    lax.fori_loop(0, 3, conv_tap, 0)
    rid = lax.broadcasted_iota(jnp.int32, (ROWS, C), 0)
    real = jnp.where(rid >= WP, rid - WP, rid) < W
    sp = latp[...] + pltpu.roll(zbuf[0], 1, 0) + zbuf[1] + pltpu.roll(zbuf[2], ROWS - 1, 0)
    zbuf[0] = jnp.where(real, sp, 0.0)
    to_groups(zbuf.at[0], snd_s)
    sp_cps = exchange(snd_s, rcv_s, a_s, a_r, 7)

    ri = lax.broadcasted_iota(jnp.int32, (UNIT, UNIT), 0)
    ci = lax.broadcasted_iota(jnp.int32, (UNIT, UNIT), 1)
    rseg = jnp.zeros((UNIT, UNIT), jnp.int32)
    cseg = jnp.zeros((UNIT, UNIT), jnp.int32)
    rid1 = lax.broadcasted_iota(jnp.int32, (UNIT, C), 0)
    nxt = jnp.zeros((UNIT, C), F32)
    prv = jnp.zeros((UNIT, C), F32)
    for f in range(16):
        rseg = jnp.where(ri // 8 == f, seg[f], rseg)
        cseg = jnp.where(ci // 8 == f, seg[f], cseg)
        if f < 15:
            ok = jnp.where(seg[f] == seg[f + 1], 1.0, 0.0).astype(F32)
            nxt = jnp.where(rid1 // 8 == f, ok, nxt)
            prv = jnp.where(rid1 // 8 == f + 1, ok, prv)
    bias = jnp.where((rseg == cseg) & (ri % 8 == ci % 8), 0.0, -1e30)
    scale = 1.0 / math.sqrt(C // HEADS)

    for cp in cot_cps:
        cp.wait_recv()
    for cp in sp_cps:
        cp.wait_recv()

    def unit(h, carry):
        spf = rcv_s[:, h].reshape(UNIT, C).astype(F32)
        cotb = rcv_c[:, h].reshape(UNIT, C)
        am = (spf * jax.nn.sigmoid(spf)).astype(BF)
        u_act[h] = am
        u_cot[h] = cotb
        tmp = spf + nn(am, wt[1])
        tmp = tmp + down8(nn(am, wt[0])) * prv
        tmp = tmp + up8(nn(am, wt[2])) * nxt
        tf = tmp.astype(BF).astype(F32)
        cen = tf - jnp.mean(tf, axis=-1, keepdims=True)
        inv = lax.rsqrt(jnp.mean(cen * cen, axis=-1, keepdims=True) + 1e-05)
        nhat = cen * inv
        nrm = nhat.astype(BF)
        u_nrm[h] = nrm
        q = nn(nrm, wq[0]).astype(BF)
        k = nn(nrm, wq[1]).astype(BF)
        v = nn(nrm, wq[2]).astype(BF)
        dm = nt(cotb, wo[...]).astype(BF)
        accs = [[None] * 3 for _ in range(4)]
        for hd in range(HEADS):
            lo, hi = 40 * hd, 40 * hd + 40
            t0, t1 = lo // 128, -(-hi // 128)
            w0, w1 = 128 * t0, 128 * t1
            lane = lax.broadcasted_iota(jnp.int32, (UNIT, w1 - w0), 1) + w0
            sel = (lane >= lo) & (lane < hi)

            def pick(t):
                return jnp.where(sel, t[:, w0:w1].astype(F32), 0.0).astype(BF)

            qm, km, vm, dmm = pick(q), pick(k), pick(v), pick(dm)
            s = nt(qm, km) * scale + bias
            e = jnp.exp(s - jnp.max(s, axis=-1, keepdims=True))
            p = e / jnp.sum(e, axis=-1, keepdims=True)
            pb = p.astype(BF)
            dpr = nt(dmm, vm)
            dsc = (p * (dpr - jnp.sum(p * dpr, axis=-1, keepdims=True)) * scale).astype(BF)
            for i, val in enumerate((nn(pb, vm), nn(dsc, km), tn(dsc, qm), tn(pb, dmm))):
                for t in range(t0, t1):
                    part = val[:, 128 * (t - t0) : 128 * (t - t0) + 128]
                    accs[i][t] = part if accs[i][t] is None else accs[i][t] + part
        mix, dq, dk, dv = (jnp.concatenate(a, axis=1) for a in accs)
        u_mix[h] = mix.astype(BF)
        dqkv = pack3(dq, dk, dv).astype(BF)
        u_dq[h] = dqkv
        dn = nt(dqkv[:, : 3 * C], wqkv[...])
        ln = inv * (
            dn
            - jnp.mean(dn, axis=-1, keepdims=True)
            - nhat * jnp.mean(dn * nhat, axis=-1, keepdims=True)
        )
        dt = (cotb.astype(F32) + ln).astype(BF)
        dtf = dt.astype(F32)
        u_dt[h] = pack3(widen(up8(dtf) * nxt), widen(dtf), widen(down8(dtf) * prv)).astype(BF)
        carried = nt(dt, wt[1]) + up8(nt(dt, wt[0])) * nxt + down8(nt(dt, wt[2])) * prv
        dsp = dtf + silu_grad(spf) * carried
        snd_d[:, h] = dsp.astype(BF).reshape(8, 16, C)
        return carry

    lax.fori_loop(0, 2, unit, 0)
    d_cps = exchange(snd_d, rcv_d, a_s, a_r, 14)

    g_t[...] = jnp.zeros_like(g_t)
    g_s[C * 3 :, :] = jnp.zeros((GR - C * 3, GL), BF)

    def both(ref):
        return jnp.concatenate([ref[0], ref[1]], axis=0)

    g_t[0:C, :] = tn(both(u_act), both(u_dt)).astype(BF)
    g_t[C : 2 * C, :] = tn(both(u_nrm), both(u_dq)).astype(BF)
    g_t[2 * C : 3 * C, 0:C] = tn(both(u_mix)[:, :C], both(u_cot)).astype(BF)

    half = GR // 2
    q1 = half // 4
    q2 = q1 // 4
    zl = GL // NZ
    mine = core * half
    other = (1 - core) * half
    base1 = mine + i1 * q1
    base2 = base1 + i2 * q2

    def r0_start(b, g):
        return [send(g.at[pl.ds(pl.multiple_of(other, 16), half)], r0.at[b],
                     s0s.at[b], s0r.at[b], sibling)]

    def r0_finish(b, g, cps):
        for cp in cps:
            cp.wait_recv()
        m = pl.ds(pl.multiple_of(mine, 16), half)
        p1[b] = (g[m, :].astype(F32) + r0[b].astype(F32)).astype(BF)

    def r1_start(b):
        cps = []
        for k in range(1, 4):
            j, peer = first_peer(k)
            cps.append(send(p1.at[b, pl.ds(pl.multiple_of(j * q1, 16), q1)], r1.at[b, k - 1],
                            s1s.at[b, k - 1], s1r.at[b, k - 1], peer))
        return cps

    def r1_finish(b, cps):
        for cp in cps:
            cp.wait_recv()
        t = p1[b, pl.ds(pl.multiple_of(i1 * q1, 16), q1), :].astype(F32)
        for k in range(3):
            t = t + r1[b, k].astype(F32)
        p2[b] = t.astype(BF)

    def r2_start(b):
        cps = []
        for k in range(1, 4):
            j, peer = second_peer(k)
            cps.append(send(p2.at[b, pl.ds(pl.multiple_of(j * q2, 16), q2)], r2.at[b, k - 1],
                            s2s.at[b, k - 1], s2r.at[b, k - 1], peer))
        return cps

    def r2_finish(b, cps):
        for cp in cps:
            cp.wait_recv()
        t = p2[b, pl.ds(pl.multiple_of(i2 * q2, 16), q2), :].astype(F32)
        for k in range(3):
            t = t + r2[b, k].astype(F32)
        t = t.astype(BF)
        for j in range(NZ):
            p3[b, j] = t[:, j * zl : (j + 1) * zl]

    def r3_start(b):
        cps = []
        for k in range(1, NZ):
            j, peer = z_peer(k)
            cps.append(send(p3.at[b, j], r3.at[b, k - 1], s3s.at[b, k - 1], s3r.at[b, k - 1], peer))
        return cps

    def r3_finish(b, f, cps):
        for cp in cps:
            cp.wait_recv()
        t = p3[b, z].astype(F32)
        for k in range(NZ - 1):
            t = t + r3[b, k].astype(F32)
        f[pl.ds(pl.multiple_of(base2, 16), q2), pl.ds(pl.multiple_of(z * zl, 128), zl)] = t.astype(BF)

    def g3_start(b, f):
        piece = f.at[pl.ds(pl.multiple_of(base2, 16), q2), pl.ds(pl.multiple_of(z * zl, 128), zl)]
        return [send(piece, piece, s3s.at[b + 2, k - 1], s3r.at[b + 2, k - 1], z_peer(k)[1])
                for k in range(1, NZ)]

    def g2_start(b, f):
        piece = f.at[pl.ds(pl.multiple_of(base2, 16), q2)]
        return [send(piece, piece, s2s.at[b + 2, k - 1], s2r.at[b + 2, k - 1], second_peer(k)[1])
                for k in range(1, 4)]

    def g1_start(b, f):
        piece = f.at[pl.ds(pl.multiple_of(base1, 16), q1)]
        return [send(piece, piece, s1s.at[b + 2, k - 1], s1r.at[b + 2, k - 1], first_peer(k)[1])
                for k in range(1, 4)]

    def g0_start(b, f):
        piece = f.at[pl.ds(pl.multiple_of(mine, 16), half)]
        return [send(piece, piece, s0s.at[b + 2], s0r.at[b + 2], sibling)]

    done = []
    t0c = r0_start(0, g_t)

    for cp in d_cps:
        cp.wait_recv()
    for g in range(14):
        t = rcv_d[g // 2, g % 2].astype(F32)
        dp[8 * g : 8 * g + 8, :] = t[:8]
        dp[WP + 8 * g : WP + 8 * g + 8, :] = t[8:]
    dv = dp[...]
    dbuf[1] = dv.astype(BF)
    dhalo = [
        send(dbuf.at[1], dbuf.at[0], dhs.at[0], dhr.at[0], row_peer(1)),
        send(dbuf.at[1], dbuf.at[2], dhs.at[1], dhr.at[1], row_peer(-1)),
    ]
    dcat = pack3(
        widen(pltpu.roll(dv, ROWS - 1, 0)), widen(dv), widen(pltpu.roll(dv, 1, 0))
    ).astype(BF)
    for a in range(3):
        g_s[a * C : (a + 1) * C, :] = tn(act[a], dcat).astype(BF)
    s0c = r0_start(1, g_s)
    r0_finish(0, g_t, t0c)
    t1c = r1_start(0)
    r0_finish(1, g_s, s0c)
    s1c = r1_start(1)

    for cp in dhalo:
        cp.wait_recv()

    @pl.when(row == 0)
    def _():
        dbuf[0] = jnp.zeros((ROWS, C), BF)

    @pl.when(row == nrow - 1)
    def _():
        dbuf[2] = jnp.zeros((ROWS, C), BF)

    def back_tap(b, carry):
        zbuf[b] = nt(dbuf[2], wsp[0, b]) + nt(dbuf[1], wsp[1, b]) + nt(dbuf[0], wsp[2, b])
        return carry

    lax.fori_loop(0, 3, back_tap, 0)
    da = pltpu.roll(zbuf[0], ROWS - 1, 0) + zbuf[1] + pltpu.roll(zbuf[2], 1, 0)
    dp[...] = dp[...] + silu_grad(latp[...]) * da
    for f in range(2):
        gin[f, 0] = dp[f * WP : f * WP + W, :].astype(BF)

    r1_finish(0, t1c)
    t2c = r2_start(0)
    r1_finish(1, s1c)
    s2c = r2_start(1)
    r2_finish(0, t2c)
    t3c = r3_start(0)
    r2_finish(1, s2c)
    s3c = r3_start(1)
    r3_finish(0, f_t, t3c)
    tg = g3_start(0, f_t)
    r3_finish(1, f_s, s3c)
    sg = g3_start(1, f_s)
    done += t0c + s0c + t1c + s1c + t2c + s2c + t3c + s3c
    for start in (g2_start, g1_start, g0_start):
        for cp in tg:
            cp.wait_recv()
        done += tg
        tg = start(0, f_t)
        for cp in sg:
            cp.wait_recv()
        done += sg
        sg = start(1, f_s)
    done += tg + sg
    outs = []
    for cps, f, o, i in ((tg, f_t, ft_out, 0), (sg, f_s, fs_out, 1)):
        for cp in cps:
            cp.wait_recv()
        cp = pltpu.make_async_copy(f, o, osem.at[i])
        cp.start()
        outs.append(cp)
    for cp in halo + cot_cps + sp_cps + d_cps + dhalo + done:
        cp.wait_send()
    for cp in outs:
        cp.wait()


def unpack(ref, r0, r1, factor):
    x = ref[r0:r1, :].astype(F32) * factor
    return x[:, :C], pltpu.roll(x[:, 256:640], CP - 64, 1)[:, :C], x[:, 640 : 640 + C]


def finish(factor, ft, fs, gs, gt, gq, go):
    for a in range(3):
        for b, t in enumerate(unpack(fs, a * C, (a + 1) * C, factor)):
            gs[a, b] = t
    for b, t in enumerate(unpack(ft, 0, C, factor)):
        gt[b] = t
    gq[...] = (ft[C : 2 * C, :].astype(F32) * factor)[:, : 3 * C]
    go[...] = (ft[2 * C : 3 * C, :].astype(F32) * factor)[:, :C]


def on_device(latents, segments, w_spatial, w_temporal, w_qkv, w_out, cotangent):
    vm = pl.BlockSpec(memory_space=pltpu.VMEM)
    anyspec = pl.BlockSpec(memory_space=pl.ANY)
    dma = pltpu.SemaphoreType.DMA
    V = pltpu.VMEM
    gin, ft, fs = pl.pallas_call(
        mega,
        out_shape=(
            jax.ShapeDtypeStruct(latents.shape, BF),
            jax.ShapeDtypeStruct((GR, GL), BF),
            jax.ShapeDtypeStruct((GR, GL), BF),
        ),
        in_specs=[pl.BlockSpec(memory_space=pltpu.SMEM), vm, vm] + [anyspec] * 4,
        out_specs=(vm, anyspec, anyspec),
        scratch_shapes=[
            V((3, 3, C, C), BF), V((3, C, C), BF), V((C, 3 * C), BF), V((3, C, CP), BF),
            V((C, C), BF), V((CP, C), BF),
            V((ROWS, C), F32), V((3, ROWS, C), BF), V((3, ROWS, C), F32),
            V((8, 2, 16, C), BF), V((8, 2, 16, C), BF), V((8, 2, 16, C), BF), V((8, 2, 16, C), BF),
            V((2, UNIT, C), BF), V((2, UNIT, GL), BF), V((2, UNIT, C), BF), V((2, UNIT, GL), BF),
            V((2, UNIT, CP), BF), V((2, UNIT, C), BF),
            V((8, 2, 16, C), BF), V((8, 2, 16, C), BF),
            V((ROWS, C), F32), V((3, ROWS, C), BF),
            V((GR, GL), BF), V((GR, GL), BF),
            V((2, GR // 2, GL), BF), V((2, 3, GR // 8, GL), BF), V((2, 3, GR // 32, GL), BF),
            V((2, NZ - 1, GR // 32, GL // NZ), BF),
            V((GR, GL), BF), V((GR, GL), BF),
            V((2, GR // 2, GL), BF), V((2, GR // 8, GL), BF), V((2, NZ, GR // 32, GL // NZ), BF),
            dma((4,)), dma((2,)), dma((2,)), dma((21,)), dma((21,)), dma((2,)), dma((2,)),
            dma((4,)), dma((4,)), dma((4, 3)), dma((4, 3)), dma((4, 3)), dma((4, 3)),
            dma((4, NZ - 1)), dma((4, NZ - 1)), dma((2,)),
        ],
        compiler_params=pltpu.CompilerParams(
            collective_id=0, has_side_effects=True, vmem_limit_bytes=56 * 1024 * 1024
        ),
        name="mega",
    )(segments, latents, cotangent, w_spatial, w_temporal, w_qkv, w_out)
    factor = 1.0 / math.sqrt(54272)
    gs, gt, gq, go = pl.pallas_call(
        lambda *refs: finish(factor, *refs),
        out_shape=(
            jax.ShapeDtypeStruct((3, 3, C, C), F32),
            jax.ShapeDtypeStruct((3, C, C), F32),
            jax.ShapeDtypeStruct((C, 3 * C), F32),
            jax.ShapeDtypeStruct((C, C), F32),
        ),
        in_specs=[vm] * 2,
        out_specs=(vm,) * 4,
        compiler_params=pltpu.CompilerParams(vmem_limit_bytes=56 * 1024 * 1024),
        name="finish",
    )(ft, fs)
    return gin, gs, gt, gq, go


def solution(mesh):
    in_specs = (
        P("frame", "row", None, None),
        P(),
        P(),
        P(),
        P(),
        P(),
        P("frame", "row", None, None),
    )
    out_specs = (P("frame", "row", None, None), P(), P(), P(), P())
    return jax.shard_map(
        on_device, mesh=mesh, in_specs=in_specs, out_specs=out_specs, check_vma=False
    )
```

time: 458 us -> 109 us (0.24)
  waiting for transfers between devices: 273 us -> 0 us
  Pallas kernels: 0 us -> 104 us
  local copies, waits for them, and re-layouts: 69.5 us -> 4.92 us
  matrix products: 49.5 us -> 0 us
  starting transfers between devices: 28.1 us -> 0 us
  other arithmetic: 21.1 us -> 0 us
  between operations: 14.8 us -> 0.64 us
    psum x1 -> x0, waiting for transfers between devices: 268 us -> none  [on_device(): lax.psum((grad_space, grad_time, grad_qkv, grad_out), ('frame', 'row'))]
    pallas_call x0 -> x2, Pallas kernels: none -> 104 us  [the longest x1 97.6 us: on_device(): pl.pallas_call(mega, out_shape=(jax.ShapeDtypeStruct(latents.shape, BF),...]
    dot_general x45 -> x0, matrix products: 45.5 us -> none  [the longest x25 16.3 us: project(): result = jnp.dot(flat, weights, preferred_element_type=jnp.float32)]
    reshape x15 -> x0, local copies, waits for them, and re-layouts: 17.4 us -> none  [the longest x11 8.98 us: project(): flat = inputs.reshape(-1, inputs.shape[-1])]
    all_to_all x3 -> x0, starting transfers between devices: 16.1 us -> none  [the longest x1 6.5 us: on_device(): lax.all_to_all(to_slots(cotangent), 'frame', split_axis=1, concat_axis=0,...]
    slice x15 -> x0, local copies, waits for them, and re-layouts: 14.4 us -> none  [the longest x7 5.76 us: conv_taps(): padded[:, tap_row:tap_row + row_count, tap_col:tap_col + col_count, :]]
    convert_element_type x12 -> x0, local copies, waits for them, and re-layouts: 13.8 us -> none  [the longest x3 3.06 us: temporal_block(): spatial_f = spatial.astype(jnp.float32)]
    ppermute x4 -> x0, starting transfers between devices: 12 us -> none  [the longest x2 9.24 us: extended(): lax.ppermute(tail, axis, [(i, (i + 1) % count) for i in range(ends)])]
  transfers between devices with their start and end apart: 8 -> 0, of which waited for: 5 -> 0; matrix products, arithmetic and copies ran while one was open for 8% -> 0% of each run, Pallas kernels for 0% -> 0%
where the time goes in v1:
time: 109 us
  Pallas kernels  104 us (95%)
  local copies, waits for them, and re-layouts  4.92 us (5%)
    pallas_call x1, Pallas kernels, on_device(): pl.pallas_call(mega, out_shape=(jax.ShapeDtypeStruct(latents.shape, BF),...  97.6 us
    pallas_call x1, Pallas kernels, on_device(): pl.pallas_call(lambda *refs: finish(factor, *refs), out_shape=(jax.ShapeD...  5.93 us
    unnamed x3, local copies, waits for them, and re-layouts  4.92 us

profile of v1, /device:TPU:1, one launch (start us, length us, event | category | flops | bytes accessed | tf_op | source)
XLA Modules:
  0.0 109.1 jit_solution(9418798425991598343)
XLA Ops:
  0.6 1.6 %copy.12.lat = bf16[2,1,106,320]{3,2,1,0:T(8,128)(2,1)} copy(bf16[2,1,106,320]{3,0,2,1:T(2,128)(2,1)} %param.7) | data formatting | bytes 271360 | tf_op args[0]
  2.2 1.6 %copy.13.cot = bf16[2,1,106,320]{3,2,1,0:T(8,128)(2,1)} copy(bf16[2,1,106,320]{3,0,2,1:T(2,128)(2,1)} %param.13) | data formatting | bytes 271360 | tf_op args[6]
  3.8 97.6 %mega.1 = (bf16[2,1,106,320]{3,2,1,0:T(8,128)(2,1)}, bf16[1024,1024]{1,0:T(8,128)(2,1)}, bf16[1024,1024]{1,0:T(8,128)(2,1)}) custom-call(s32[16]{0:T(128)} %seg.1, bf16[2,1,106,320]{3,2,1,0:T(8,128)(2,1)} %copy.12.lat, bf16[2,1,106,320]{3,2,1,0:T(8,128)(2,1)} %copy.13.cot, bf16[3,3,320,320]{3,2,1,0:T(8,128)(2,1)} %wsp_h.1, bf16[3,320,320]{2,1,0:T(8,128)(2,1)} %wt_h.1, ...), custom_call_target="tpu_custom_call" | custom-call | tf_op jit(solution)/shard_map/mega/pallas_call | solution.py:478
  101.5 1.7 %copy.14 = bf16[2,1,106,320]{3,0,2,1:T(2,128)(2,1)} copy(bf16[2,1,106,320]{3,2,1,0:T(8,128)(2,1)} %get-tuple-element.19) | data formatting | bytes 271360
  103.2 5.9 %finish.1 = (f32[3,3,320,320]{3,2,1,0:T(8,128)}, f32[3,320,320]{2,1,0:T(8,128)}, f32[320,960]{1,0:T(8,128)}, f32[320,320]{1,0:T(8,128)}) custom-call(bf16[1024,1024]{1,0:T(8,128)(2,1)} %get-tuple-element.13.refs_0_, bf16[1024,1024]{1,0:T(8,128)(2,1)} %get-tuple-element.14.refs_1_), custom_call_target="tpu_custom_call" | custom-call | tf_op jit(solution)/shard_map/finish/pallas_call | solution.py:511

commit v2 on v1

v2 whole, which is shorter than its diff:
```python
import math

import jax
import jax.numpy as jnp
from jax import lax
from jax.experimental import pallas as pl
from jax.experimental.pallas import tpu as pltpu
from jax.sharding import PartitionSpec as P

MESH = pl.DeviceIdType.MESH
BF = jnp.bfloat16
F32 = jnp.float32
HEADS = 8
C = 320
CP = 384
W = 106
WP = 112
ROWS = 2 * WP
UNIT = 128
NR = (768, 960)
GL = 1024
NX, NY, NZ = 4, 4, 8


def nn(a, b):
    return lax.dot_general(a, b, (((1,), (0,)), ((), ())), preferred_element_type=F32)


def nt(a, b):
    return lax.dot_general(a, b, (((1,), (1,)), ((), ())), preferred_element_type=F32)


def tn(a, b):
    return lax.dot_general(a, b, (((0,), (0,)), ((), ())), preferred_element_type=F32)


def widen(x):
    return jnp.concatenate([x, jnp.zeros((x.shape[0], CP - C), x.dtype)], axis=1)


def pack3(a, b, c):
    b = pltpu.roll(b, 64, 1)
    return jnp.concatenate([a[:, :256], a[:, 256:] + b[:, :128], b[:, 128:], c], axis=1)


def silu_grad(v):
    sig = jax.nn.sigmoid(v)
    return sig * (1.0 + v * (1.0 - sig))


def up8(x):
    return jnp.concatenate([x[8:], jnp.zeros((8, x.shape[1]), x.dtype)], axis=0)


def down8(x):
    return jnp.concatenate([jnp.zeros((8, x.shape[1]), x.dtype), x[:-8]], axis=0)


OUT_BLOCKS = (
    [(640, 256 * j + 128 * r, 128 * r, 128 * j, 128) for j in range(3) for r in range(2)]
    + [(640, 768, 256, 0, 64), (704, 768, 256, 128, 64), (640, 896, 256, 256, 64)]
)


def mega(
    seg_h, lat, cot, wsp_h, wt_h, wqkv_h, wout_h,
    gi, f_t, f_s,
    seg, wsp, wt, wqkv, wq, wtr, wout, wo,
    latn, latp, act, zbuf, snd_s, snd_c, rcv_s, rcv_c,
    u_act, u_dt, u_nrm, u_dq, u_mix, u_cot, snd_d, rcv_d,
    dp, dbuf, g_t, g_s, r0, r1, r2, r3, p1, p2, p3, g3,
    wsem, hs, hr, a_s, a_r, dhs, dhr, s0s, s0r, s1s, s1r, s2s, s2r, s3s, s3r,
):
    fr, row = lax.axis_index("frame"), lax.axis_index("row")
    y, core = fr // 2, fr % 2
    z, x = row // NX, row % NX
    nrow = NX * NZ

    def at(yy, cc, zz, xx):
        return {"frame": yy * 2 + cc, "row": zz * NX + xx}

    def frame_peer(k):
        return {"frame": lax.rem(fr + k, 8), "row": row}

    def row_peer(k):
        return {"frame": fr, "row": lax.rem(row + k + nrow, nrow)}

    i1 = jnp.where(core == 0, x, y)
    i2 = jnp.where(core == 0, y, x)

    def first_peer(k):
        j = lax.rem(i1 + k, 4)
        return j, at(jnp.where(core == 0, y, j), core, z, jnp.where(core == 0, j, x))

    def second_peer(k):
        j = lax.rem(i2 + k, 4)
        return j, at(jnp.where(core == 0, j, y), core, z, jnp.where(core == 0, x, j))

    def z_peer(k):
        j = lax.rem(z + k, NZ)
        return j, at(y, core, j, x)

    sibling = at(y, 1 - core, z, x)

    barrier = pltpu.get_barrier_semaphore()
    peers = [z_peer(k)[1] for k in range(1, NZ)]
    peers += [frame_peer(k) for k in range(1, 8)]
    peers += [row_peer(1), row_peer(-1)]
    peers += [at(y, core, z, lax.rem(x + k, NX)) for k in range(1, NX)]
    for peer in peers:
        pl.semaphore_signal(barrier, inc=1, device_id=peer, device_id_type=MESH)

    loads = [
        pltpu.make_async_copy(s, d, wsem.at[i])
        for i, (s, d) in enumerate(
            [(lat, latn.at[0]), (cot, latn.at[1]), (wqkv_h, wqkv), (wout_h, wout), (wsp_h, wsp), (wt_h, wt), (seg_h, seg)]
        )
    ]
    for cp in loads:
        cp.start()

    def send(src, dst, ssem, rsem, peer):
        cp = pltpu.make_async_remote_copy(
            src_ref=src, dst_ref=dst, send_sem=ssem, recv_sem=rsem,
            device_id=peer, device_id_type=MESH,
        )
        cp.start()
        return cp

    latp[...] = jnp.zeros_like(latp)
    dp[...] = jnp.zeros_like(dp)

    def rows_of(i, dst):
        loads[i].wait()
        v = latn[i].astype(F32)
        for f in range(2):
            dst[f * WP : f * WP + W, :] = v[:, f, :]

    rows_of(0, latp)
    lv = latp[...]
    act[1] = (lv * jax.nn.sigmoid(lv)).astype(BF)

    def to_groups(src, dst):
        for g in range(16):
            if g < 14:
                t = jnp.concatenate(
                    [src[8 * g : 8 * g + 8, :], src[WP + 8 * g : WP + 8 * g + 8, :]], axis=0
                )
            else:
                t = jnp.zeros((16, C), F32)
            dst[g // 2, g % 2] = t.astype(BF)

    pl.semaphore_wait(barrier, len(peers))

    halo = [
        send(act.at[1], act.at[0], hs.at[0], hr.at[0], row_peer(1)),
        send(act.at[1], act.at[2], hs.at[1], hr.at[1], row_peer(-1)),
    ]

    def exchange(snd, rcv, ssem, rsem, base):
        cps = []
        for k in range(1, 8):
            cps.append(
                send(snd.at[lax.rem(fr + k, 8)], rcv.at[fr],
                     ssem.at[base + k - 1], rsem.at[base + k - 1], frame_peer(k))
            )
        rcv[pl.ds(fr, 1)] = snd[pl.ds(fr, 1)]
        return cps

    rows_of(1, dp)
    to_groups(dp, snd_c)
    cot_cps = exchange(snd_c, rcv_c, a_s, a_r, 0)

    for cp in loads[2:]:
        cp.wait()
    wo[...] = jnp.zeros_like(wo)
    wo[:C, :] = wout[...]
    for i in range(3):
        if i == 1:
            t = pltpu.roll(wqkv[:, 256:640].astype(F32), CP - 64, 1).astype(BF)
        else:
            t = wqkv[:, 640 * (i // 2) : 640 * (i // 2) + C]
        t = widen(t[:, :C])
        wq[i] = t
        if i > 0:
            wtr[i - 1] = t.T

    ri = lax.broadcasted_iota(jnp.int32, (UNIT, UNIT), 0)
    ci = lax.broadcasted_iota(jnp.int32, (UNIT, UNIT), 1)
    rseg = jnp.zeros((UNIT, UNIT), jnp.int32)
    cseg = jnp.zeros((UNIT, UNIT), jnp.int32)
    nxt = jnp.zeros((UNIT, UNIT), F32)
    prv = jnp.zeros((UNIT, UNIT), F32)
    for f in range(16):
        rseg = jnp.where(ri // 8 == f, seg[f], rseg)
        cseg = jnp.where(ci // 8 == f, seg[f], cseg)
        if f < 15:
            ok = jnp.where(seg[f] == seg[f + 1], 1.0, 0.0).astype(F32)
            nxt = jnp.where(ri // 8 == f, ok, nxt)
            prv = jnp.where(ri // 8 == f + 1, ok, prv)
    bias = jnp.where((rseg == cseg) & (ri % 8 == ci % 8), 0.0, -1e30)

    def wide(m):
        m = jnp.concatenate([m, m, m], axis=1)[:, :C]
        return jnp.concatenate([m, m], axis=0)

    nxt, prv = wide(nxt), wide(prv)
    scale = 1.0 / math.sqrt(C // HEADS)

    for cp in halo:
        cp.wait_recv()

    @pl.when(row == 0)
    def _():
        act[0] = jnp.zeros((ROWS, C), BF)

    @pl.when(row == nrow - 1)
    def _():
        act[2] = jnp.zeros((ROWS, C), BF)

    for b in range(3):
        zbuf[b] = nn(act[0], wsp[0, b]) + nn(act[1], wsp[1, b]) + nn(act[2], wsp[2, b])
    rid = lax.broadcasted_iota(jnp.int32, (ROWS, C), 0)
    real = jnp.where(rid >= WP, rid - WP, rid) < W
    sp = latp[...] + pltpu.roll(zbuf[0], 1, 0) + zbuf[1] + pltpu.roll(zbuf[2], ROWS - 1, 0)
    zbuf[0] = jnp.where(real, sp, 0.0)
    to_groups(zbuf.at[0], snd_s)
    sp_cps = exchange(snd_s, rcv_s, a_s, a_r, 7)

    for cp in cot_cps:
        cp.wait_recv()
    for cp in sp_cps:
        cp.wait_recv()

    def both(ref):
        return jnp.concatenate([ref[:, h].reshape(UNIT, C) for h in range(2)], axis=0)

    spf = both(rcv_s).astype(F32)
    cotb = both(rcv_c)
    am = (spf * jax.nn.sigmoid(spf)).astype(BF)
    u_act[...] = am
    u_cot[...] = cotb
    tmp = spf + nn(am, wt[1])
    tmp = tmp + down8(nn(am, wt[0])) * prv
    tmp = tmp + up8(nn(am, wt[2])) * nxt
    tf = tmp.astype(BF).astype(F32)
    cen = tf - jnp.mean(tf, axis=-1, keepdims=True)
    inv = lax.rsqrt(jnp.mean(cen * cen, axis=-1, keepdims=True) + 1e-05)
    nhat = cen * inv
    nrm = nhat.astype(BF)
    u_nrm[...] = nrm
    qall = nn(nrm, wq[0]).astype(BF)
    kall = nn(nrm, wq[1]).astype(BF)
    vall = nn(nrm, wq[2]).astype(BF)
    kt = nt(wtr[0], nrm)
    vt = nt(wtr[1], nrm)
    dmall = nt(cotb, wo[...]).astype(BF)

    def attention(u):
        rows = slice(UNIT * u, UNIT * u + UNIT)
        state, mixt, dqt = [], [], []
        dk, dv = [None] * 3, [None] * 3
        for hd in range(HEADS):
            lo, hi = 40 * hd, 40 * hd + 40
            t0, t1 = lo // 128, -(-hi // 128)
            w0, w1 = 128 * t0, 128 * t1
            lane = lax.broadcasted_iota(jnp.int32, (UNIT, w1 - w0), 1) + w0
            sel = (lane >= lo) & (lane < hi)
            qm = jnp.where(sel, qall[rows, w0:w1].astype(F32), 0.0).astype(BF)
            dmm = jnp.where(sel, dmall[rows, w0:w1].astype(F32), 0.0).astype(BF)
            state.append((lo, hi, t0, t1, qm, dmm, nt(kall[rows, w0:w1], qm), nt(vall[rows, w0:w1], dmm)))
        second = []
        for lo, hi, t0, t1, qm, dmm, s, dpr in state:
            s = s * scale + bias
            e = jnp.exp(s - jnp.max(s, axis=0, keepdims=True))
            p = e * (1.0 / jnp.sum(e, axis=0, keepdims=True))
            ds = (p * (dpr - jnp.sum(p * dpr, axis=0, keepdims=True)) * scale).astype(BF)
            second.append((lo, hi, t0, t1, qm, dmm, p.astype(BF), ds))
        for lo, hi, t0, t1, qm, dmm, pb, ds in second:
            mixt.append(nn(vt[lo:hi, rows].astype(BF), pb))
            dqt.append(nn(kt[lo:hi, rows].astype(BF), ds))
            for acc, val in ((dk, nn(ds, qm)), (dv, nn(pb, dmm))):
                for t in range(t0, t1):
                    part = val[:, 128 * (t - t0) : 128 * (t - t0) + 128]
                    acc[t] = part if acc[t] is None else acc[t] + part
        u_mix[:, rows] = jnp.concatenate(mixt, axis=0).astype(BF)
        dq = widen(jnp.concatenate(dqt, axis=0).T)
        u_dq[rows, :] = pack3(dq, jnp.concatenate(dk, axis=1), jnp.concatenate(dv, axis=1)).astype(BF)

    attention(0)
    attention(1)
    dn = nt(u_dq[:, : 3 * C], wqkv[...])
    ln = inv * (
        dn
        - jnp.mean(dn, axis=-1, keepdims=True)
        - nhat * jnp.mean(dn * nhat, axis=-1, keepdims=True)
    )
    dt = (cotb.astype(F32) + ln).astype(BF)
    dtf = dt.astype(F32)
    carried = nt(dt, wt[1]) + up8(nt(dt, wt[0])) * nxt + down8(nt(dt, wt[2])) * prv
    dsp = (dtf + silu_grad(spf) * carried).astype(BF)
    for h in range(2):
        snd_d[:, h] = dsp[UNIT * h : UNIT * h + UNIT].reshape(8, 16, C)
    d_cps = exchange(snd_d, rcv_d, a_s, a_r, 14)

    u_dt[...] = pack3(widen(up8(dtf) * nxt), widen(dtf), widen(down8(dtf) * prv)).astype(BF)
    g_t[0:C, :] = tn(u_act[...], u_dt[...]).astype(BF)
    g_t[C : 2 * C, :] = tn(u_nrm[...], u_dq[...]).astype(BF)
    go = widen(nn(u_mix[...], u_cot[...])).astype(BF)
    g_t[2 * C : 2 * C + 128, 768:] = jnp.zeros((128, 256), BF)
    for dst, lane, src, col, n in OUT_BLOCKS:
        g_t[dst : dst + n, lane : lane + 128] = go[src : src + n, col : col + 128]

    bufs = (g_t, g_s)
    outs = (f_t, f_s)
    half = [n // 2 for n in NR]
    quar = [n // 4 for n in NR]
    mine = [pl.multiple_of(core * n, 16) for n in half]
    other = [pl.multiple_of((1 - core) * n, 16) for n in half]
    low = [pl.multiple_of(i2 // 2 * n, 16) for n in quar]
    lane1 = pl.multiple_of(i1 * 256, 256)
    lane2 = pl.multiple_of(i2 % 2 * 128, 128)

    def r0_start(b):
        return [
            send(bufs[b].at[pl.ds(other[b], half[b]), pl.ds(256 * j, 256)],
                 r0.at[b, pl.ds(0, half[b]), pl.ds(256 * j, 256)], s0s.at[b, j], s0r.at[b, j], sibling)
            for j in range(4)
        ]

    def r0_finish(b, cps):
        for j, cp in enumerate(cps):
            cp.wait_recv()
            sl = slice(256 * j, 256 * j + 256)
            p1[b, : half[b], sl] = (
                bufs[b][pl.ds(mine[b], half[b]), sl].astype(F32) + r0[b, : half[b], sl].astype(F32)
            ).astype(BF)

    def r1_start(b):
        cps = []
        for k in range(1, 4):
            j, peer = first_peer(k)
            cps.append(
                send(p1.at[b, pl.ds(0, half[b]), pl.ds(pl.multiple_of(j * 256, 256), 256)],
                     r1.at[b, k - 1, pl.ds(0, half[b])], s1s.at[b, k - 1], s1r.at[b, k - 1], peer)
            )
        return cps

    def r1_finish(b, cps):
        for cp in cps:
            cp.wait_recv()
        t = p1[b, : half[b], pl.ds(lane1, 256)].astype(F32)
        for k in range(3):
            t = t + r1[b, k, : half[b]].astype(F32)
        p2[b, : half[b]] = t.astype(BF)

    def r2_start(b):
        cps = []
        for k in range(1, 4):
            j, peer = second_peer(k)
            cps.append(
                send(p2.at[b, pl.ds(pl.multiple_of(j // 2 * quar[b], 16), quar[b]),
                           pl.ds(pl.multiple_of(j % 2 * 128, 128), 128)],
                     r2.at[b, k - 1, pl.ds(0, quar[b])], s2s.at[b, k - 1], s2r.at[b, k - 1], peer)
            )
        return cps

    def r2_finish(b, cps):
        for cp in cps:
            cp.wait_recv()
        t = p2[b, pl.ds(low[b], quar[b]), pl.ds(lane2, 128)].astype(F32)
        for k in range(3):
            t = t + r2[b, k, : quar[b]].astype(F32)
        p3[b, : quar[b]] = t.astype(BF)
        p3[b, quar[b] :] = jnp.zeros((256 - quar[b], 128), BF)

    def r3_start(b):
        cps = []
        for k in range(1, NZ):
            j, peer = z_peer(k)
            cps.append(
                send(p3.at[b, pl.ds(pl.multiple_of(j * 32, 32), 32)], r3.at[b, k - 1],
                     s3s.at[b, k - 1], s3r.at[b, k - 1], peer)
            )
        return cps

    zrow = pl.multiple_of(z * 32, 32)

    def r3_finish(b, cps):
        for cp in cps:
            cp.wait_recv()
        t = p3[b, pl.ds(zrow, 32)].astype(F32)
        for k in range(NZ - 1):
            t = t + r3[b, k].astype(F32)
        g3[b, pl.ds(zrow, 32)] = t.astype(BF)

    def g3_start(b):
        piece = g3.at[b, pl.ds(zrow, 32)]
        return [
            send(piece, piece, s3s.at[b + 2, k - 1], s3r.at[b + 2, k - 1], z_peer(k)[1])
            for k in range(1, NZ)
        ]

    def g3_finish(b, cps):
        for cp in cps:
            cp.wait_recv()
        outs[b][pl.ds(pl.multiple_of(mine[b] + low[b], 16), quar[b]),
                pl.ds(pl.multiple_of(lane1 + lane2, 128), 128)] = g3[b, : quar[b]]

    def g2_start(b):
        piece = outs[b].at[pl.ds(pl.multiple_of(mine[b] + low[b], 16), quar[b]),
                           pl.ds(pl.multiple_of(lane1 + lane2, 128), 128)]
        return [
            send(piece, piece, s2s.at[b + 2, k - 1], s2r.at[b + 2, k - 1], second_peer(k)[1])
            for k in range(1, 4)
        ]

    def block(b, j):
        return outs[b].at[pl.ds(mine[b], half[b]), pl.ds(pl.multiple_of(j * 256, 256), 256)]

    def g1_start(b):
        piece = block(b, i1)
        return [
            send(piece, piece, s1s.at[b + 2, k - 1], s1r.at[b + 2, k - 1], first_peer(k)[1])
            for k in range(1, 4)
        ]

    def g0_start(b, k):
        piece = block(b, lax.rem(i1 - k + 4, 4))
        return send(piece, piece, s0s.at[b + 2, k], s0r.at[b + 2, k], sibling)

    def got(cps):
        for cp in cps:
            cp.wait_recv()

    sent = []

    def keep(cps):
        sent.extend(cps)
        return cps

    t0c = keep(r0_start(0))
    r0_finish(0, t0c)
    t1c = keep(r1_start(0))

    got(d_cps)
    for g in range(14):
        t = rcv_d[g // 2, g % 2].astype(F32)
        dp[8 * g : 8 * g + 8, :] = t[:8]
        dp[WP + 8 * g : WP + 8 * g + 8, :] = t[8:]
    dv = dp[...]
    dbuf[1] = dv.astype(BF)
    dcat = pack3(
        widen(pltpu.roll(dv, ROWS - 1, 0)), widen(dv), widen(pltpu.roll(dv, 1, 0))
    ).astype(BF)
    for a in range(3):
        g_s[a * C : (a + 1) * C, :] = tn(act[a], dcat).astype(BF)
    s0c = keep(r0_start(1))
    r0_finish(1, s0c)
    s1c = keep(r1_start(1))
    dhalo = [
        send(dbuf.at[1], dbuf.at[0], dhs.at[0], dhr.at[0], row_peer(1)),
        send(dbuf.at[1], dbuf.at[2], dhs.at[1], dhr.at[1], row_peer(-1)),
    ]
    r1_finish(0, t1c)
    t2c = keep(r2_start(0))
    r2_finish(0, t2c)
    t3c = keep(r3_start(0))
    r1_finish(1, s1c)
    s2c = keep(r2_start(1))
    r3_finish(0, t3c)
    t4c = keep(g3_start(0))
    r2_finish(1, s2c)
    s3c = keep(r3_start(1))

    got(dhalo)

    @pl.when(row == 0)
    def _():
        dbuf[0] = jnp.zeros((ROWS, C), BF)

    @pl.when(row == nrow - 1)
    def _():
        dbuf[2] = jnp.zeros((ROWS, C), BF)

    for b in range(3):
        zbuf[b] = nt(dbuf[2], wsp[0, b]) + nt(dbuf[1], wsp[1, b]) + nt(dbuf[0], wsp[2, b])
    da = pltpu.roll(zbuf[0], ROWS - 1, 0) + zbuf[1] + pltpu.roll(zbuf[2], 1, 0)
    gi[...] = (dp[...] + silu_grad(latp[...]) * da).astype(BF)

    g3_finish(0, t4c)
    t5c = keep(g2_start(0))
    r3_finish(1, s3c)
    s4c = keep(g3_start(1))
    got(t5c)
    t6c = keep(g1_start(0))
    g3_finish(1, s4c)
    s5c = keep(g2_start(1))
    got(s5c)
    s6c = keep(g1_start(1))
    s7c = [g0_start(1, 0)]
    t7c = [g0_start(0, 0)]
    for k in range(1, 4):
        t6c[k - 1].wait_recv()
        t7c.append(g0_start(0, k))
    for k in range(1, 4):
        s6c[k - 1].wait_recv()
        s7c.append(g0_start(1, k))
    keep(t7c + s7c)
    got(t7c)
    got(s7c)
    for cp in halo + cot_cps + sp_cps + d_cps + dhalo + sent:
        cp.wait_send()


def unpack(x):
    return x[:, :C], pltpu.roll(x[:, 256:640], CP - 64, 1)[:, :C], x[:, 640 : 640 + C]


def finish(factor, gi, ft, fs, gin, gs, gt, gq, go, vs, vt, vq, vo, vi, sem):
    cps = []

    def out(src, dst):
        cp = pltpu.make_async_copy(src, dst, sem.at[len(cps)])
        cp.start()
        cps.append(cp)

    for a in range(3):
        for b, t in enumerate(unpack(fs[a * C : (a + 1) * C, :].astype(F32) * factor)):
            vs[a, b] = t
        out(vs.at[a], gs.at[a])
    for b, t in enumerate(unpack(ft[0:C, :].astype(F32) * factor)):
        vt[b] = t
    out(vt, gt)
    vq[...] = (ft[C : 2 * C, :].astype(F32) * factor)[:, : 3 * C]
    out(vq, gq)
    for dst, lane, src, col, n in OUT_BLOCKS:
        w = min(128, C - col)
        vo[src : src + n, col : col + w] = ft[dst : dst + n, lane : lane + w].astype(F32) * factor
    out(vo, go)
    g = gi[...].astype(F32)
    vi[...] = jnp.stack([g[:W], g[WP : WP + W]], axis=1).astype(BF)
    out(vi, gin)
    for cp in cps:
        cp.wait()


def on_device(latents, segments, w_spatial, w_temporal, w_qkv, w_out, cotangent):
    vm = pl.BlockSpec(memory_space=pltpu.VMEM)
    anyspec = pl.BlockSpec(memory_space=pl.ANY)
    dma = pltpu.SemaphoreType.DMA
    V = pltpu.VMEM
    hm, qm = max(NR) // 2, max(NR) // 4

    def by_column(t):
        return jnp.transpose(t.reshape(2, W, C), (1, 0, 2))

    gi, ft, fs = pl.pallas_call(
        mega,
        out_shape=(
            jax.ShapeDtypeStruct((ROWS, C), BF),
            jax.ShapeDtypeStruct((NR[0], GL), BF),
            jax.ShapeDtypeStruct((NR[1], GL), BF),
        ),
        in_specs=[pl.BlockSpec(memory_space=pltpu.HBM)] * 7,
        out_specs=(vm, vm, vm),
        scratch_shapes=[
            pltpu.SMEM((16,), jnp.int32), V((3, 3, C, C), BF), V((3, C, C), BF), V((C, 3 * C), BF), V((3, C, CP), BF),
            V((2, CP, C), BF), V((C, C), BF), V((CP, C), BF),
            V((2, W, 2, C), BF), V((ROWS, C), F32), V((3, ROWS, C), BF), V((3, ROWS, C), F32),
            V((8, 2, 16, C), BF), V((8, 2, 16, C), BF), V((8, 2, 16, C), BF), V((8, 2, 16, C), BF),
            V((2 * UNIT, C), BF), V((2 * UNIT, GL), BF), V((2 * UNIT, C), BF), V((2 * UNIT, GL), BF),
            V((C, 2 * UNIT), BF), V((2 * UNIT, C), BF),
            V((8, 2, 16, C), BF), V((8, 2, 16, C), BF),
            V((ROWS, C), F32), V((3, ROWS, C), BF),
            V((NR[0], GL), BF), V((NR[1], GL), BF),
            V((2, hm, GL), BF), V((2, 3, hm, 256), BF), V((2, 3, qm, 128), BF),
            V((2, NZ - 1, 32, 128), BF),
            V((2, hm, GL), BF), V((2, hm, 256), BF), V((2, 256, 128), BF), V((2, 256, 128), BF),
            dma((7,)), dma((2,)), dma((2,)), dma((21,)), dma((21,)), dma((2,)), dma((2,)),
            dma((4, 4)), dma((4, 4)), dma((4, 3)), dma((4, 3)), dma((4, 3)), dma((4, 3)),
            dma((4, NZ - 1)), dma((4, NZ - 1)),
        ],
        compiler_params=pltpu.CompilerParams(
            collective_id=0, has_side_effects=True, vmem_limit_bytes=40 * 1024 * 1024
        ),
        name="mega",
    )(*(
        pltpu.with_memory_space_constraint(t, pltpu.HBM)
        for t in (segments, by_column(latents), by_column(cotangent), w_spatial, w_temporal, w_qkv, w_out)
    ))
    factor = 1.0 / math.sqrt(54272)
    shapes = [(3, 3, C, C), (3, C, C), (C, 3 * C), (C, C)]
    gin, gs, gt, gq, go = pl.pallas_call(
        lambda *refs: finish(factor, *refs),
        out_shape=(jax.ShapeDtypeStruct((W, 2, C), BF),)
        + tuple(jax.ShapeDtypeStruct(s, F32) for s in shapes),
        in_specs=[vm] * 3,
        out_specs=(anyspec,) * 5,
        scratch_shapes=[V(s, F32) for s in shapes] + [V((W, 2, C), BF), dma((7,))],
        compiler_params=pltpu.CompilerParams(vmem_limit_bytes=40 * 1024 * 1024),
        name="finish",
    )(gi, ft, fs)
    gin = jnp.transpose(gin, (1, 0, 2)).reshape(latents.shape)
    return gin, gs, gt, gq, go


def solution(mesh):
    in_specs = (
        P("frame", "row", None, None),
        P(),
        P(),
        P(),
        P(),
        P(),
        P("frame", "row", None, None),
    )
    out_specs = (P("frame", "row", None, None), P(), P(), P(), P())
    return jax.shard_map(
        on_device, mesh=mesh, in_specs=in_specs, out_specs=out_specs, check_vma=False
    )
```

time: 109 us -> 84.5 us (0.78)
  Pallas kernels: 104 us -> 83.4 us
  local copies, waits for them, and re-layouts: 4.92 us -> 0 us
    pallas_call x1, Pallas kernels: 97.6 us -> 79.9 us  [on_device(): pl.pallas_call(mega, out_shape=(jax.ShapeDtypeStruct((ROWS, C), BF), jax....]
    unnamed x3 -> x0, local copies, waits for them, and re-layouts: 4.92 us -> none
    pallas_call x1, Pallas kernels: 5.93 us -> 3.46 us  [on_device(): pl.pallas_call(lambda *refs: finish(factor, *refs), out_shape=(jax.ShapeD...]
where the time goes in v2:
time: 84.5 us; the launch traced here: 84 us
  Pallas kernels  83.4 us (99%)
    pallas_call x1, Pallas kernels, on_device(): pl.pallas_call(mega, out_shape=(jax.ShapeDtypeStruct((ROWS, C), BF), jax....  79.9 us
    pallas_call x1, Pallas kernels, on_device(): pl.pallas_call(lambda *refs: finish(factor, *refs), out_shape=(jax.ShapeD...  3.46 us

profile of v2, /device:TPU:1, one launch (start us, length us, event | category | flops | bytes accessed | tf_op | source)
XLA Modules:
  0.0 84.0 jit_solution(6084289313672056134)
XLA Ops:
  0.6 79.9 %mega.1 = (bf16[224,320]{1,0:T(8,128)(2,1)S(1)}, bf16[768,1024]{1,0:T(8,128)(2,1)S(1)}, bf16[960,1024]{1,0:T(8,128)(2,1)S(1)}) custom-call(s32[16]{0:T(128)} %seg_h.1, bf16[106,2,320]{2,1,0:T(2,128)(2,1)} %bitcast.9, bf16[106,2,320]{2,1,0:T(2,128)(2,1)} %bitcast.10, bf16[3,3,320,320]{3,2,1,0:T(8,128)(2,1)} %wsp_h.1, bf16[3,320,320]{2,1,0:T(8,128)(2,1)} %wt_h.1, ...), custom_call_target="tpu_custom_call" | custom-call | tf_op jit(solution)/shard_map/mega/pallas_call | solution.py:558
  80.6 3.5 %finish.1 = (bf16[106,2,320]{2,1,0:T(2,128)(2,1)}, f32[3,3,320,320]{3,2,1,0:T(8,128)}, f32[3,320,320]{2,1,0:T(8,128)}, f32[320,960]{1,0:T(8,128)}, f32[320,320]{1,0:T(8,128)}) custom-call(bf16[224,320]{1,0:T(8,128)(2,1)S(1)} %get-tuple-element.13.refs_0_, bf16[768,1024]{1,0:T(8,128)(2,1)S(1)} %get-tuple-element.14.refs_1_, ...), custom_call_target="tpu_custom_call" | custom-call | tf_op jit(solution)/shard_map/finish/pallas_call | solution.py:594

commit v3 on v2

--- a/solution.py
+++ b/solution.py
@@ -56,19 +56,40 @@
     return jnp.concatenate([jnp.zeros((8, x.shape[1]), x.dtype), x[:-8]], axis=0)
 
 
+NEAR_LAST = {4: (2, 1, 3), 8: (4, 3, 5, 2, 6, 1, 7)}
+
+
+def pack2(v):
+    r = v.shape[0] // 2
+    t = widen(v)[:, 256:]
+    return jnp.concatenate([v[:r, :256], v[r:, :256], t[:r] + pltpu.roll(t[r:], 64, 1)], axis=1)
+
+
+def unpack2(v):
+    t = v[:, 512:].astype(F32)
+    lo = jnp.concatenate([v[:, :256], t.astype(BF)[:, :64]], axis=1)
+    hi = jnp.concatenate([v[:, 256:512], pltpu.roll(t, 64, 1).astype(BF)[:, :64]], axis=1)
+    return jnp.concatenate([lo, hi], axis=0)
+
+
 OUT_BLOCKS = (
     [(640, 256 * j + 128 * r, 128 * r, 128 * j, 128) for j in range(3) for r in range(2)]
     + [(640, 768, 256, 0, 64), (704, 768, 256, 128, 64), (640, 896, 256, 256, 64)]
 )
 
 
+def unpack(x):
+    return x[:, :C], pltpu.roll(x[:, 256:640], CP - 64, 1)[:, :C], x[:, 640 : 640 + C]
+
+
 def mega(
+    factor,
     seg_h, lat, cot, wsp_h, wt_h, wqkv_h, wout_h,
-    gi, f_t, f_s,
+    gi, out_t, out_q, out_o, f_s,
     seg, wsp, wt, wqkv, wq, wtr, wout, wo,
-    latn, latp, act, zbuf, snd_s, snd_c, rcv_s, rcv_c,
+    latn, latp, act, hbuf, dhb, zbuf, snd_s, snd_c, rcv_s, rcv_c,
     u_act, u_dt, u_nrm, u_dq, u_mix, u_cot, snd_d, rcv_d,
-    dp, dbuf, g_t, g_s, r0, r1, r2, r3, p1, p2, p3, g3,
+    dp, dbuf, g_t, g_s, r0, r1, r2, r3, p1, p2, p3, g3, f_t,
     wsem, hs, hr, a_s, a_r, dhs, dhr, s0s, s0r, s1s, s1r, s2s, s2r, s3s, s3r,
 ):
     fr, row = lax.axis_index("frame"), lax.axis_index("row")
@@ -103,8 +124,8 @@
     sibling = at(y, 1 - core, z, x)
 
     barrier = pltpu.get_barrier_semaphore()
-    peers = [z_peer(k)[1] for k in range(1, NZ)]
-    peers += [frame_peer(k) for k in range(1, 8)]
+    peers = [z_peer(k)[1] for k in NEAR_LAST[NZ]]
+    peers += [frame_peer(k) for k in NEAR_LAST[8]]
     peers += [row_peer(1), row_peer(-1)]
     peers += [at(y, core, z, lax.rem(x + k, NX)) for k in range(1, NX)]
     for peer in peers:
@@ -138,28 +159,31 @@
 
     rows_of(0, latp)
     lv = latp[...]
-    act[1] = (lv * jax.nn.sigmoid(lv)).astype(BF)
-
-    def to_groups(src, dst):
-        for g in range(16):
-            if g < 14:
-                t = jnp.concatenate(
-                    [src[8 * g : 8 * g + 8, :], src[WP + 8 * g : WP + 8 * g + 8, :]], axis=0
-                )
-            else:
-                t = jnp.zeros((16, C), F32)
-            dst[g // 2, g % 2] = t.astype(BF)
+    lv = lv * jax.nn.sigmoid(lv)
+    act[1] = lv.astype(BF)
+    hbuf[1] = pack2(lv).astype(BF)
+
+    def to_pixels(src, dst):
+        halves = [
+            jnp.concatenate(
+                [src[WP * f + 16 * j + 8 * h : WP * f + 16 * j + 8 * h + 8, :] for j in range(7) for f in range(2)]
+                + [jnp.zeros((16, C), F32)],
+                axis=0,
+            )
+            for h in range(2)
+        ]
+        dst[...] = pack2(jnp.concatenate(halves, axis=0)).astype(BF).reshape(8, 16, 2 * C)
 
     pl.semaphore_wait(barrier, len(peers))
 
     halo = [
-        send(act.at[1], act.at[0], hs.at[0], hr.at[0], row_peer(1)),
-        send(act.at[1], act.at[2], hs.at[1], hr.at[1], row_peer(-1)),
+        send(hbuf.at[1], hbuf.at[0], hs.at[0], hr.at[0], row_peer(1)),
+        send(hbuf.at[1], hbuf.at[2], hs.at[1], hr.at[1], row_peer(-1)),
     ]
 
     def exchange(snd, rcv, ssem, rsem, base):
         cps = []
-        for k in range(1, 8):
+        for k in NEAR_LAST[8]:
             cps.append(
                 send(snd.at[lax.rem(fr + k, 8)], rcv.at[fr],
                      ssem.at[base + k - 1], rsem.at[base + k - 1], frame_peer(k))
@@ -168,11 +192,39 @@
         return cps
 
     rows_of(1, dp)
-    to_groups(dp, snd_c)
+    to_pixels(dp, snd_c)
     cot_cps = exchange(snd_c, rcv_c, a_s, a_r, 0)
 
-    for cp in loads[2:]:
-        cp.wait()
+    loads[4].wait()
+    for b in range(3):
+        zbuf[b] = nn(act[1], wsp[1, b])
+    for cp in halo:
+        cp.wait_recv()
+
+    def edges(ref):
+        @pl.when(row == 0)
+        def _():
+            ref[0] = jnp.zeros((WP, 2 * C), BF)
+
+        @pl.when(row == nrow - 1)
+        def _():
+            ref[2] = jnp.zeros((WP, 2 * C), BF)
+
+    edges(hbuf)
+    act[0] = unpack2(hbuf[0])
+    act[2] = unpack2(hbuf[2])
+
+    for b in range(3):
+        zbuf[b] += nn(act[0], wsp[0, b]) + nn(act[2], wsp[2, b])
+    rid = lax.broadcasted_iota(jnp.int32, (ROWS, C), 0)
+    real = jnp.where(rid >= WP, rid - WP, rid) < W
+    sp = latp[...] + pltpu.roll(zbuf[0], 1, 0) + zbuf[1] + pltpu.roll(zbuf[2], ROWS - 1, 0)
+    zbuf[0] = jnp.where(real, sp, 0.0)
+    to_pixels(zbuf.at[0], snd_s)
+    sp_cps = exchange(snd_s, rcv_s, a_s, a_r, 7)
+
+    for i in (2, 3, 5, 6):
+        loads[i].wait()
     wo[...] = jnp.zeros_like(wo)
     wo[:C, :] = wout[...]
     for i in range(3):
@@ -207,36 +259,13 @@
     nxt, prv = wide(nxt), wide(prv)
     scale = 1.0 / math.sqrt(C // HEADS)
 
-    for cp in halo:
-        cp.wait_recv()
-
-    @pl.when(row == 0)
-    def _():
-        act[0] = jnp.zeros((ROWS, C), BF)
-
-    @pl.when(row == nrow - 1)
-    def _():
-        act[2] = jnp.zeros((ROWS, C), BF)
-
-    for b in range(3):
-        zbuf[b] = nn(act[0], wsp[0, b]) + nn(act[1], wsp[1, b]) + nn(act[2], wsp[2, b])
-    rid = lax.broadcasted_iota(jnp.int32, (ROWS, C), 0)
-    real = jnp.where(rid >= WP, rid - WP, rid) < W
-    sp = latp[...] + pltpu.roll(zbuf[0], 1, 0) + zbuf[1] + pltpu.roll(zbuf[2], ROWS - 1, 0)
-    zbuf[0] = jnp.where(real, sp, 0.0)
-    to_groups(zbuf.at[0], snd_s)
-    sp_cps = exchange(snd_s, rcv_s, a_s, a_r, 7)
-
     for cp in cot_cps:
         cp.wait_recv()
     for cp in sp_cps:
         cp.wait_recv()
 
-    def both(ref):
-        return jnp.concatenate([ref[:, h].reshape(UNIT, C) for h in range(2)], axis=0)
-
-    spf = both(rcv_s).astype(F32)
-    cotb = both(rcv_c)
+    spf = unpack2(rcv_s[...].reshape(UNIT, 2 * C)).astype(F32)
+    cotb = unpack2(rcv_c[...].reshape(UNIT, 2 * C))
     am = (spf * jax.nn.sigmoid(spf)).astype(BF)
     u_act[...] = am
     u_cot[...] = cotb
@@ -298,9 +327,7 @@
     dt = (cotb.astype(F32) + ln).astype(BF)
     dtf = dt.astype(F32)
     carried = nt(dt, wt[1]) + up8(nt(dt, wt[0])) * nxt + down8(nt(dt, wt[2])) * prv
-    dsp = (dtf + silu_grad(spf) * carried).astype(BF)
-    for h in range(2):
-        snd_d[:, h] = dsp[UNIT * h : UNIT * h + UNIT].reshape(8, 16, C)
+    snd_d[...] = pack2(dtf + silu_grad(spf) * carried).astype(BF).reshape(8, 16, 2 * C)
     d_cps = exchange(snd_d, rcv_d, a_s, a_r, 14)
 
     u_dt[...] = pack3(widen(up8(dtf) * nxt), widen(dtf), widen(down8(dtf) * prv)).astype(BF)
@@ -321,24 +348,28 @@
     lane1 = pl.multiple_of(i1 * 256, 256)
     lane2 = pl.multiple_of(i2 % 2 * 128, 128)
 
-    def r0_start(b):
+    third = [n // 3 for n in half]
+
+    def r0_start(b, c):
+        rows = third[b]
         return [
-            send(bufs[b].at[pl.ds(other[b], half[b]), pl.ds(256 * j, 256)],
-                 r0.at[b, pl.ds(0, half[b]), pl.ds(256 * j, 256)], s0s.at[b, j], s0r.at[b, j], sibling)
-            for j in range(4)
+            send(bufs[b].at[pl.ds(pl.multiple_of(other[b] + c * rows, 16), rows), pl.ds(512 * j, 512)],
+                 r0.at[b, pl.ds(c * rows, rows), pl.ds(512 * j, 512)],
+                 s0s.at[b, 2 * c + j], s0r.at[b, 2 * c + j], sibling)
+            for j in range(2)
         ]
 
-    def r0_finish(b, cps):
-        for j, cp in enumerate(cps):
+    def r0_finish(b, c, cps):
+        for cp in cps:
             cp.wait_recv()
-            sl = slice(256 * j, 256 * j + 256)
-            p1[b, : half[b], sl] = (
-                bufs[b][pl.ds(mine[b], half[b]), sl].astype(F32) + r0[b, : half[b], sl].astype(F32)
-            ).astype(BF)
+        rows = third[b]
+        m = pl.ds(pl.multiple_of(mine[b] + c * rows, 16), rows)
+        sl = slice(c * rows, c * rows + rows)
+        p1[b, sl] = (bufs[b][m, :].astype(F32) + r0[b, sl].astype(F32)).astype(BF)
 
     def r1_start(b):
         cps = []
-        for k in range(1, 4):
+        for k in NEAR_LAST[4]:
             j, peer = first_peer(k)
             cps.append(
                 send(p1.at[b, pl.ds(0, half[b]), pl.ds(pl.multiple_of(j * 256, 256), 256)],
@@ -356,7 +387,7 @@
 
     def r2_start(b):
         cps = []
-        for k in range(1, 4):
+        for k in NEAR_LAST[4]:
             j, peer = second_peer(k)
             cps.append(
                 send(p2.at[b, pl.ds(pl.multiple_of(j // 2 * quar[b], 16), quar[b]),
@@ -376,7 +407,7 @@
 
     def r3_start(b):
         cps = []
-        for k in range(1, NZ):
+        for k in NEAR_LAST[NZ]:
             j, peer = z_peer(k)
             cps.append(
                 send(p3.at[b, pl.ds(pl.multiple_of(j * 32, 32), 32)], r3.at[b, k - 1],
@@ -398,7 +429,7 @@
         piece = g3.at[b, pl.ds(zrow, 32)]
         return [
             send(piece, piece, s3s.at[b + 2, k - 1], s3r.at[b + 2, k - 1], z_peer(k)[1])
-            for k in range(1, NZ)
+            for k in NEAR_LAST[NZ]
         ]
 
     def g3_finish(b, cps):
@@ -412,7 +443,7 @@
                            pl.ds(pl.multiple_of(lane1 + lane2, 128), 128)]
         return [
             send(piece, piece, s2s.at[b + 2, k - 1], s2r.at[b + 2, k - 1], second_peer(k)[1])
-            for k in range(1, 4)
+            for k in NEAR_LAST[4]
         ]
 
     def block(b, j):
@@ -422,12 +453,17 @@
         piece = block(b, i1)
         return [
             send(piece, piece, s1s.at[b + 2, k - 1], s1r.at[b + 2, k - 1], first_peer(k)[1])
-            for k in range(1, 4)
+            for k in NEAR_LAST[4]
         ]
 
     def g0_start(b, k):
-        piece = block(b, lax.rem(i1 - k + 4, 4))
-        return send(piece, piece, s0s.at[b + 2, k], s0r.at[b + 2, k], sibling)
+        lanes = pl.ds(pl.multiple_of(lax.rem(i1 - k + 4, 4) * 256, 256), 256)
+        cps = []
+        for c in range(3):
+            rows = pl.ds(pl.multiple_of(mine[b] + c * third[b], 16), third[b])
+            piece = outs[b].at[rows, lanes]
+            cps.append(send(piece, piece, s0s.at[b + 2, 3 * k + c], s0r.at[b + 2, 3 * k + c], sibling))
+        return cps
 
     def got(cps):
         for cp in cps:
@@ -439,57 +475,64 @@
         sent.extend(cps)
         return cps
 
-    t0c = keep(r0_start(0))
-    r0_finish(0, t0c)
+    t0c = [keep(r0_start(0, c)) for c in range(3)]
+    for c in range(3):
+        r0_finish(0, c, t0c[c])
     t1c = keep(r1_start(0))
 
     got(d_cps)
-    for g in range(14):
-        t = rcv_d[g // 2, g % 2].astype(F32)
-        dp[8 * g : 8 * g + 8, :] = t[:8]
-        dp[WP + 8 * g : WP + 8 * g + 8, :] = t[8:]
-    dv = dp[...]
+    t = unpack2(rcv_d[...].reshape(UNIT, 2 * C)).astype(F32)
+    dv = jnp.concatenate(
+        [
+            t[UNIT * h + 16 * j + 8 * f : UNIT * h + 16 * j + 8 * f + 8]
+            for f in range(2) for j in range(7) for h in range(2)
+        ],
+        axis=0,
+    )
+    dp[...] = dv
     dbuf[1] = dv.astype(BF)
+    dhb[1] = pack2(dv).astype(BF)
     dcat = pack3(
         widen(pltpu.roll(dv, ROWS - 1, 0)), widen(dv), widen(pltpu.roll(dv, 1, 0))
     ).astype(BF)
+    s0c = []
     for a in range(3):
-        g_s[a * C : (a + 1) * C, :] = tn(act[a], dcat).astype(BF)
-    s0c = keep(r0_start(1))
-    r0_finish(1, s0c)
+        t = tn(act[a], dcat).astype(BF)
+        for c in range(2):
+            g_s[c * half[1] + a * 160 : c * half[1] + a * 160 + 160, :] = t[160 * c : 160 * c + 160]
+        s0c.append(keep(r0_start(1, a)))
+    for a in range(3):
+        r0_finish(1, a, s0c[a])
     s1c = keep(r1_start(1))
-    dhalo = [
-        send(dbuf.at[1], dbuf.at[0], dhs.at[0], dhr.at[0], row_peer(1)),
-        send(dbuf.at[1], dbuf.at[2], dhs.at[1], dhr.at[1], row_peer(-1)),
-    ]
     r1_finish(0, t1c)
     t2c = keep(r2_start(0))
     r2_finish(0, t2c)
     t3c = keep(r3_start(0))
     r1_finish(1, s1c)
     s2c = keep(r2_start(1))
+    dhalo = [
+        send(dhb.at[1], dhb.at[0], dhs.at[0], dhr.at[0], row_peer(1)),
+        send(dhb.at[1], dhb.at[2], dhs.at[1], dhr.at[1], row_peer(-1)),
+    ]
     r3_finish(0, t3c)
     t4c = keep(g3_start(0))
     r2_finish(1, s2c)
     s3c = keep(r3_start(1))
+    g3_finish(0, t4c)
+    t5c = keep(g2_start(0))
 
     got(dhalo)
 
-    @pl.when(row == 0)
-    def _():
-        dbuf[0] = jnp.zeros((ROWS, C), BF)
-
-    @pl.when(row == nrow - 1)
-    def _():
-        dbuf[2] = jnp.zeros((ROWS, C), BF)
+    edges(dhb)
+    dbuf[0] = unpack2(dhb[0])
+    dbuf[2] = unpack2(dhb[2])
 
     for b in range(3):
         zbuf[b] = nt(dbuf[2], wsp[0, b]) + nt(dbuf[1], wsp[1, b]) + nt(dbuf[0], wsp[2, b])
     da = pltpu.roll(zbuf[0], ROWS - 1, 0) + zbuf[1] + pltpu.roll(zbuf[2], 1, 0)
-    gi[...] = (dp[...] + silu_grad(latp[...]) * da).astype(BF)
-
-    g3_finish(0, t4c)
-    t5c = keep(g2_start(0))
+    t = dp[...] + silu_grad(latp[...]) * da
+    gi[...] = jnp.stack([t[:W], t[WP : WP + W]], axis=1).astype(BF)
+
     r3_finish(1, s3c)
     s4c = keep(g3_start(1))
     got(t5c)
@@ -498,26 +541,28 @@
     s5c = keep(g2_start(1))
     got(s5c)
     s6c = keep(g1_start(1))
-    s7c = [g0_start(1, 0)]
-    t7c = [g0_start(0, 0)]
-    for k in range(1, 4):
-        t6c[k - 1].wait_recv()
-        t7c.append(g0_start(0, k))
-    for k in range(1, 4):
-        s6c[k - 1].wait_recv()
-        s7c.append(g0_start(1, k))
+    s7c = g0_start(1, 0)
+    t7c = g0_start(0, 0)
+    for cp, k in zip(t6c, NEAR_LAST[4]):
+        cp.wait_recv()
+        t7c += g0_start(0, k)
+    got(t7c)
+    for b, t in enumerate(unpack(f_t[0:C, :].astype(F32) * factor)):
+        out_t[b] = t
+    out_q[...] = (f_t[C : 2 * C, :].astype(F32) * factor)[:, : 3 * C]
+    for dst, lane, src, col, n in OUT_BLOCKS:
+        w = min(128, C - col)
+        out_o[src : src + n, col : col + w] = f_t[dst : dst + n, lane : lane + w].astype(F32) * factor
+    for cp, k in zip(s6c, NEAR_LAST[4]):
+        cp.wait_recv()
+        s7c += g0_start(1, k)
     keep(t7c + s7c)
-    got(t7c)
     got(s7c)
     for cp in halo + cot_cps + sp_cps + d_cps + dhalo + sent:
         cp.wait_send()
 
 
-def unpack(x):
-    return x[:, :C], pltpu.roll(x[:, 256:640], CP - 64, 1)[:, :C], x[:, 640 : 640 + C]
-
-
-def finish(factor, gi, ft, fs, gin, gs, gt, gq, go, vs, vt, vq, vo, vi, sem):
+def finish(factor, gi, vt, vq, vo, fs, gin, gs, gt, gq, go, vs, sem):
     cps = []
 
     def out(src, dst):
@@ -525,22 +570,20 @@
         cp.start()
         cps.append(cp)
 
+    for b in range(3):
+        out(vt.at[b], gt.at[b])
+    for i in range(4):
+        r = slice(80 * i, 80 * i + 80)
+        out(vq.at[r], gq.at[r])
+    out(vo, go)
+    out(gi, gin)
     for a in range(3):
-        for b, t in enumerate(unpack(fs[a * C : (a + 1) * C, :].astype(F32) * factor)):
-            vs[a, b] = t
-        out(vs.at[a], gs.at[a])
-    for b, t in enumerate(unpack(ft[0:C, :].astype(F32) * factor)):
-        vt[b] = t
-    out(vt, gt)
-    vq[...] = (ft[C : 2 * C, :].astype(F32) * factor)[:, : 3 * C]
-    out(vq, gq)
-    for dst, lane, src, col, n in OUT_BLOCKS:
-        w = min(128, C - col)
-        vo[src : src + n, col : col + w] = ft[dst : dst + n, lane : lane + w].astype(F32) * factor
-    out(vo, go)
-    g = gi[...].astype(F32)
-    vi[...] = jnp.stack([g[:W], g[WP : WP + W]], axis=1).astype(BF)
-    out(vi, gin)
+        for c in range(2):
+            r = c * (NR[1] // 2) + 160 * a
+            for b, t in enumerate(unpack(fs[r : r + 160, :].astype(F32) * factor)):
+                vs[a, b, 160 * c : 160 * c + 160, :] = t
+        for b in range(3):
+            out(vs.at[a, b], gs.at[a, b])
     for cp in cps:
         cp.wait()
 
@@ -555,30 +598,32 @@
     def by_column(t):
         return jnp.transpose(t.reshape(2, W, C), (1, 0, 2))
 
-    gi, ft, fs = pl.pallas_call(
-        mega,
-        out_shape=(
-            jax.ShapeDtypeStruct((ROWS, C), BF),
-            jax.ShapeDtypeStruct((NR[0], GL), BF),
-            jax.ShapeDtypeStruct((NR[1], GL), BF),
-        ),
+    factor = 1.0 / math.sqrt(54272)
+    shapes = [(3, 3, C, C), (3, C, C), (C, 3 * C), (C, C)]
+    inner = pl.pallas_call(
+        lambda *refs: mega(factor, *refs),
+        out_shape=(jax.ShapeDtypeStruct((W, 2, C), BF),)
+        + tuple(jax.ShapeDtypeStruct(s, F32) for s in shapes[1:])
+        + (jax.ShapeDtypeStruct((NR[1], GL), BF),),
         in_specs=[pl.BlockSpec(memory_space=pltpu.HBM)] * 7,
-        out_specs=(vm, vm, vm),
+        out_specs=(vm,) * 5,
         scratch_shapes=[
             pltpu.SMEM((16,), jnp.int32), V((3, 3, C, C), BF), V((3, C, C), BF), V((C, 3 * C), BF), V((3, C, CP), BF),
             V((2, CP, C), BF), V((C, C), BF), V((CP, C), BF),
-            V((2, W, 2, C), BF), V((ROWS, C), F32), V((3, ROWS, C), BF), V((3, ROWS, C), F32),
-            V((8, 2, 16, C), BF), V((8, 2, 16, C), BF), V((8, 2, 16, C), BF), V((8, 2, 16, C), BF),
+            V((2, W, 2, C), BF), V((ROWS, C), F32), V((3, ROWS, C), BF),
+            V((3, WP, 2 * C), BF), V((3, WP, 2 * C), BF), V((3, ROWS, C), F32),
+            V((8, 16, 2 * C), BF), V((8, 16, 2 * C), BF), V((8, 16, 2 * C), BF), V((8, 16, 2 * C), BF),
             V((2 * UNIT, C), BF), V((2 * UNIT, GL), BF), V((2 * UNIT, C), BF), V((2 * UNIT, GL), BF),
             V((C, 2 * UNIT), BF), V((2 * UNIT, C), BF),
-            V((8, 2, 16, C), BF), V((8, 2, 16, C), BF),
+            V((8, 16, 2 * C), BF), V((8, 16, 2 * C), BF),
             V((ROWS, C), F32), V((3, ROWS, C), BF),
             V((NR[0], GL), BF), V((NR[1], GL), BF),
             V((2, hm, GL), BF), V((2, 3, hm, 256), BF), V((2, 3, qm, 128), BF),
             V((2, NZ - 1, 32, 128), BF),
             V((2, hm, GL), BF), V((2, hm, 256), BF), V((2, 256, 128), BF), V((2, 256, 128), BF),
+            V((NR[0], GL), BF),
             dma((7,)), dma((2,)), dma((2,)), dma((21,)), dma((21,)), dma((2,)), dma((2,)),
-            dma((4, 4)), dma((4, 4)), dma((4, 3)), dma((4, 3)), dma((4, 3)), dma((4, 3)),
+            dma((4, 12)), dma((4, 12)), dma((4, 3)), dma((4, 3)), dma((4, 3)), dma((4, 3)),
             dma((4, NZ - 1)), dma((4, NZ - 1)),
         ],
         compiler_params=pltpu.CompilerParams(
@@ -589,18 +634,16 @@
         pltpu.with_memory_space_constraint(t, pltpu.HBM)
         for t in (segments, by_column(latents), by_column(cotangent), w_spatial, w_temporal, w_qkv, w_out)
     ))
-    factor = 1.0 / math.sqrt(54272)
-    shapes = [(3, 3, C, C), (3, C, C), (C, 3 * C), (C, C)]
     gin, gs, gt, gq, go = pl.pallas_call(
         lambda *refs: finish(factor, *refs),
         out_shape=(jax.ShapeDtypeStruct((W, 2, C), BF),)
         + tuple(jax.ShapeDtypeStruct(s, F32) for s in shapes),
-        in_specs=[vm] * 3,
+        in_specs=[vm] * 5,
         out_specs=(anyspec,) * 5,
-        scratch_shapes=[V(s, F32) for s in shapes] + [V((W, 2, C), BF), dma((7,))],
+        scratch_shapes=[V(shapes[0], F32), dma((18,))],
         compiler_params=pltpu.CompilerParams(vmem_limit_bytes=40 * 1024 * 1024),
         name="finish",
-    )(gi, ft, fs)
+    )(*inner)
     gin = jnp.transpose(gin, (1, 0, 2)).reshape(latents.shape)
     return gin, gs, gt, gq, go
 

time: 84.5 us -> 76.6 us (0.907)
  Pallas kernels: 83.4 us -> 75.7 us
    pallas_call x1, Pallas kernels: 79.9 us -> 72.4 us  [on_device(): pl.pallas_call(lambda *refs: mega(factor, *refs), out_shape=(jax.ShapeDty...]
where the time goes in v3:
time: 76.6 us; the launch traced here: 76.5 us
  Pallas kernels  75.7 us (99%)
  between operations  0.8 us (1%)
    pallas_call x1, Pallas kernels, on_device(): pl.pallas_call(lambda *refs: mega(factor, *refs), out_shape=(jax.ShapeDty...  72.4 us
    pallas_call x1, Pallas kernels, on_device(): pl.pallas_call(lambda *refs: finish(factor, *refs), out_shape=(jax.ShapeD...  3.28 us

profile of v3, /device:TPU:1, one launch (start us, length us, event | category | flops | bytes accessed | tf_op | source)
XLA Modules:
  0.0 76.5 jit_solution(2809413469478758539)
XLA Ops:
  0.6 72.4 %mega.1 = (bf16[106,2,320]{2,1,0:T(2,128)(2,1)S(1)}, f32[3,320,320]{2,1,0:T(8,128)S(1)}, f32[320,960]{1,0:T(8,128)S(1)}, f32[320,320]{1,0:T(8,128)S(1)}, bf16[960,1024]{1,0:T(8,128)(2,1)S(1)}) custom-call(s32[16]{0:T(128)} %refs_0_.1, bf16[106,2,320]{2,1,0:T(2,128)(2,1)} %bitcast.9, bf16[106,2,320]{2,1,0:T(2,128)(2,1)} %bitcast.10, ...), custom_call_target="tpu_custom_call" | custom-call | tf_op jit(solution)/shard_map/mega/pallas_call | solution.py:603
  73.0 3.3 %finish.1 = (bf16[106,2,320]{2,1,0:T(2,128)(2,1)}, f32[3,3,320,320]{3,2,1,0:T(8,128)}, f32[3,320,320]{2,1,0:T(8,128)}, f32[320,960]{1,0:T(8,128)}, f32[320,320]{1,0:T(8,128)}) custom-call(bf16[106,2,320]{2,1,0:T(2,128)(2,1)S(1)} %get-tuple-element.15.refs_0_, f32[3,320,320]{2,1,0:T(8,128)S(1)} %get-tuple-element.16.refs_1_, ...), custom_call_target="tpu_custom_call" | custom-call | tf_op jit(solution)/shard_map/finish/pallas_call | solution.py:637

commit v4 on v3

--- a/solution.py
+++ b/solution.py
@@ -72,6 +72,9 @@
     return jnp.concatenate([lo, hi], axis=0)
 
 
+MAIN = 384
+REST = 96
+
 OUT_BLOCKS = (
     [(640, 256 * j + 128 * r, 128 * r, 128 * j, 128) for j in range(3) for r in range(2)]
     + [(640, 768, 256, 0, 64), (704, 768, 256, 128, 64), (640, 896, 256, 256, 64)]
@@ -89,8 +92,8 @@
     seg, wsp, wt, wqkv, wq, wtr, wout, wo,
     latn, latp, act, hbuf, dhb, zbuf, snd_s, snd_c, rcv_s, rcv_c,
     u_act, u_dt, u_nrm, u_dq, u_mix, u_cot, snd_d, rcv_d,
-    dp, dbuf, g_t, g_s, r0, r1, r2, r3, p1, p2, p3, g3, f_t,
-    wsem, hs, hr, a_s, a_r, dhs, dhr, s0s, s0r, s1s, s1r, s2s, s2r, s3s, s3r,
+    dp, dbuf, g_t, g_s, r0, r1, r2, r3, p1, p2, p3, g3, f_t, zr, zx, zy,
+    wsem, hs, hr, a_s, a_r, dhs, dhr, s0s, s0r, s1s, s1r, s2s, s2r, s3s, s3r, zs, zv,
 ):
     fr, row = lax.axis_index("frame"), lax.axis_index("row")
     y, core = fr // 2, fr % 2
@@ -341,7 +344,7 @@
     bufs = (g_t, g_s)
     outs = (f_t, f_s)
     half = [n // 2 for n in NR]
-    quar = [n // 4 for n in NR]
+    quar = [MAIN // 2] * 2
     mine = [pl.multiple_of(core * n, 16) for n in half]
     other = [pl.multiple_of((1 - core) * n, 16) for n in half]
     low = [pl.multiple_of(i2 // 2 * n, 16) for n in quar]
@@ -372,18 +375,18 @@
         for k in NEAR_LAST[4]:
             j, peer = first_peer(k)
             cps.append(
-                send(p1.at[b, pl.ds(0, half[b]), pl.ds(pl.multiple_of(j * 256, 256), 256)],
-                     r1.at[b, k - 1, pl.ds(0, half[b])], s1s.at[b, k - 1], s1r.at[b, k - 1], peer)
+                send(p1.at[b, pl.ds(0, MAIN), pl.ds(pl.multiple_of(j * 256, 256), 256)],
+                     r1.at[b, k - 1, pl.ds(0, MAIN)], s1s.at[b, k - 1], s1r.at[b, k - 1], peer)
             )
         return cps
 
     def r1_finish(b, cps):
         for cp in cps:
             cp.wait_recv()
-        t = p1[b, : half[b], pl.ds(lane1, 256)].astype(F32)
+        t = p1[b, : MAIN, pl.ds(lane1, 256)].astype(F32)
         for k in range(3):
-            t = t + r1[b, k, : half[b]].astype(F32)
-        p2[b, : half[b]] = t.astype(BF)
+            t = t + r1[b, k, : MAIN].astype(F32)
+        p2[b, : MAIN] = t.astype(BF)
 
     def r2_start(b):
         cps = []
@@ -447,7 +450,7 @@
         ]
 
     def block(b, j):
-        return outs[b].at[pl.ds(mine[b], half[b]), pl.ds(pl.multiple_of(j * 256, 256), 256)]
+        return outs[b].at[pl.ds(mine[b], MAIN), pl.ds(pl.multiple_of(j * 256, 256), 256)]
 
     def g1_start(b):
         piece = block(b, i1)
@@ -460,7 +463,7 @@
         lanes = pl.ds(pl.multiple_of(lax.rem(i1 - k + 4, 4) * 256, 256), 256)
         cps = []
         for c in range(3):
-            rows = pl.ds(pl.multiple_of(mine[b] + c * third[b], 16), third[b])
+            rows = pl.ds(pl.multiple_of(mine[b] + c * (MAIN // 3), 16), MAIN // 3)
             piece = outs[b].at[rows, lanes]
             cps.append(send(piece, piece, s0s.at[b + 2, 3 * k + c], s0r.at[b + 2, 3 * k + c], sibling))
         return cps
@@ -468,6 +471,53 @@
     def got(cps):
         for cp in cps:
             cp.wait_recv()
+
+    zlane = pl.multiple_of(z * 128, 128)
+    rest = pl.ds(pl.multiple_of(mine[1] + MAIN, 16), REST)
+
+    def z1_start():
+        cps = []
+        for k in NEAR_LAST[NZ]:
+            j, peer = z_peer(k)
+            cps.append(
+                send(p1.at[1, pl.ds(MAIN, REST), pl.ds(pl.multiple_of(j * 128, 128), 128)],
+                     zr.at[k - 1], zs.at[0, k - 1], zv.at[0, k - 1], peer)
+            )
+        return cps
+
+    def z1_finish(cps):
+        got(cps)
+        t = p1[1, MAIN : MAIN + REST, pl.ds(zlane, 128)].astype(F32)
+        for k in range(NZ - 1):
+            t = t + zr[k].astype(F32)
+        zx[pl.ds(i1, 1)] = t.astype(BF)[None]
+
+    def spread(ref, place, sem, peer_of):
+        piece = ref.at[place]
+        return [
+            send(piece, piece, zs.at[sem, k - 1], zv.at[sem, k - 1], peer_of(k)[1])
+            for k in NEAR_LAST[4]
+        ]
+
+    def in_order(ref):
+        t = ref[0].astype(F32)
+        for k in range(1, 4):
+            t = t + ref[k].astype(F32)
+        return t.astype(BF)
+
+    def z4_start():
+        piece = f_s.at[rest, pl.ds(zlane, 128)]
+        return [
+            send(piece, piece, zs.at[3, k - 1], zv.at[3, k - 1], z_peer(k)[1])
+            for k in NEAR_LAST[NZ]
+        ]
+
+    def z0_start():
+        cps = []
+        for j in range(2):
+            piece = f_s.at[rest, pl.ds(512 * j, 512)]
+            cps.append(send(piece, piece, s0s.at[3, 12 + j], s0r.at[3, 12 + j], sibling))
+        return cps
 
     sent = []
 
@@ -504,6 +554,7 @@
     for a in range(3):
         r0_finish(1, a, s0c[a])
     s1c = keep(r1_start(1))
+    z1c = keep(z1_start())
     r1_finish(0, t1c)
     t2c = keep(r2_start(0))
     r2_finish(0, t2c)
@@ -514,10 +565,15 @@
         send(dhb.at[1], dhb.at[0], dhs.at[0], dhr.at[0], row_peer(1)),
         send(dhb.at[1], dhb.at[2], dhs.at[1], dhr.at[1], row_peer(-1)),
     ]
+    z1_finish(z1c)
+    z2c = keep(spread(zx, i1, 1, first_peer))
     r3_finish(0, t3c)
     t4c = keep(g3_start(0))
     r2_finish(1, s2c)
     s3c = keep(r3_start(1))
+    got(z2c)
+    zy[pl.ds(i2, 1)] = in_order(zx)[None]
+    z3c = keep(spread(zy, i2, 2, second_peer))
     g3_finish(0, t4c)
     t5c = keep(g2_start(0))
 
@@ -535,10 +591,13 @@
 
     r3_finish(1, s3c)
     s4c = keep(g3_start(1))
+    got(z3c)
+    f_s[rest, pl.ds(zlane, 128)] = in_order(zy)
     got(t5c)
     t6c = keep(g1_start(0))
     g3_finish(1, s4c)
     s5c = keep(g2_start(1))
+    z4c = keep(z4_start())
     got(s5c)
     s6c = keep(g1_start(1))
     s7c = g0_start(1, 0)
@@ -546,6 +605,11 @@
     for cp, k in zip(t6c, NEAR_LAST[4]):
         cp.wait_recv()
         t7c += g0_start(0, k)
+    got(z4c)
+    s7c += z0_start()
+    for cp, k in zip(s6c, NEAR_LAST[4]):
+        cp.wait_recv()
+        s7c += g0_start(1, k)
     got(t7c)
     for b, t in enumerate(unpack(f_t[0:C, :].astype(F32) * factor)):
         out_t[b] = t
@@ -553,9 +617,6 @@
     for dst, lane, src, col, n in OUT_BLOCKS:
         w = min(128, C - col)
         out_o[src : src + n, col : col + w] = f_t[dst : dst + n, lane : lane + w].astype(F32) * factor
-    for cp, k in zip(s6c, NEAR_LAST[4]):
-        cp.wait_recv()
-        s7c += g0_start(1, k)
     keep(t7c + s7c)
     got(s7c)
     for cp in halo + cot_cps + sp_cps + d_cps + dhalo + sent:
@@ -593,7 +654,7 @@
     anyspec = pl.BlockSpec(memory_space=pl.ANY)
     dma = pltpu.SemaphoreType.DMA
     V = pltpu.VMEM
-    hm, qm = max(NR) // 2, max(NR) // 4
+    hm = max(NR) // 2
 
     def by_column(t):
         return jnp.transpose(t.reshape(2, W, C), (1, 0, 2))
@@ -618,13 +679,13 @@
             V((8, 16, 2 * C), BF), V((8, 16, 2 * C), BF),
             V((ROWS, C), F32), V((3, ROWS, C), BF),
             V((NR[0], GL), BF), V((NR[1], GL), BF),
-            V((2, hm, GL), BF), V((2, 3, hm, 256), BF), V((2, 3, qm, 128), BF),
+            V((2, hm, GL), BF), V((2, 3, MAIN, 256), BF), V((2, 3, MAIN // 2, 128), BF),
             V((2, NZ - 1, 32, 128), BF),
-            V((2, hm, GL), BF), V((2, hm, 256), BF), V((2, 256, 128), BF), V((2, 256, 128), BF),
-            V((NR[0], GL), BF),
+            V((2, hm, GL), BF), V((2, MAIN, 256), BF), V((2, 256, 128), BF), V((2, 256, 128), BF),
+            V((NR[0], GL), BF), V((NZ - 1, REST, 128), BF), V((4, REST, 128), BF), V((4, REST, 128), BF),
             dma((7,)), dma((2,)), dma((2,)), dma((21,)), dma((21,)), dma((2,)), dma((2,)),
-            dma((4, 12)), dma((4, 12)), dma((4, 3)), dma((4, 3)), dma((4, 3)), dma((4, 3)),
-            dma((4, NZ - 1)), dma((4, NZ - 1)),
+            dma((4, 14)), dma((4, 14)), dma((4, 3)), dma((4, 3)), dma((4, 3)), dma((4, 3)),
+            dma((4, NZ - 1)), dma((4, NZ - 1)), dma((4, NZ - 1)), dma((4, NZ - 1)),
         ],
         compiler_params=pltpu.CompilerParams(
             collective_id=0, has_side_effects=True, vmem_limit_bytes=40 * 1024 * 1024

time: 76.6 us -> 75.5 us (0.986)
  Pallas kernels: 75.7 us -> 74.6 us
    pallas_call x1, Pallas kernels: 72.4 us -> 71.3 us  [on_device(): pl.pallas_call(lambda *refs: mega(factor, *refs), out_shape=(jax.ShapeDty...]
where the time goes in v4:
time: 75.5 us; the launch traced here: 75.4 us
  Pallas kernels  74.6 us (99%)
  between operations  0.8 us (1%)
    pallas_call x1, Pallas kernels, on_device(): pl.pallas_call(lambda *refs: mega(factor, *refs), out_shape=(jax.ShapeDty...  71.3 us
    pallas_call x1, Pallas kernels, on_device(): pl.pallas_call(lambda *refs: finish(factor, *refs), out_shape=(jax.ShapeD...  3.28 us

profile of v4, /device:TPU:1, one launch (start us, length us, event | category | flops | bytes accessed | tf_op | source)
XLA Modules:
  0.0 75.4 jit_solution(5867050829021300954)
XLA Ops:
  0.6 71.3 %mega.1 = (bf16[106,2,320]{2,1,0:T(2,128)(2,1)S(1)}, f32[3,320,320]{2,1,0:T(8,128)S(1)}, f32[320,960]{1,0:T(8,128)S(1)}, f32[320,320]{1,0:T(8,128)S(1)}, bf16[960,1024]{1,0:T(8,128)(2,1)S(1)}) custom-call(s32[16]{0:T(128)} %refs_0_.1, bf16[106,2,320]{2,1,0:T(2,128)(2,1)} %bitcast.9, bf16[106,2,320]{2,1,0:T(2,128)(2,1)} %bitcast.10, ...), custom_call_target="tpu_custom_call" | custom-call | tf_op jit(solution)/shard_map/mega/pallas_call | solution.py:664
  72.0 3.3 %finish.1 = (bf16[106,2,320]{2,1,0:T(2,128)(2,1)}, f32[3,3,320,320]{3,2,1,0:T(8,128)}, f32[3,320,320]{2,1,0:T(8,128)}, f32[320,960]{1,0:T(8,128)}, f32[320,320]{1,0:T(8,128)}) custom-call(bf16[106,2,320]{2,1,0:T(2,128)(2,1)S(1)} %get-tuple-element.15.refs_0_, f32[3,320,320]{2,1,0:T(8,128)S(1)} %get-tuple-element.16.refs_1_, ...), custom_call_target="tpu_custom_call" | custom-call | tf_op jit(solution)/shard_map/finish/pallas_call | solution.py:698

commit v5 on v4

--- a/solution.py
+++ b/solution.py
@@ -541,7 +541,6 @@
     )
     dp[...] = dv
     dbuf[1] = dv.astype(BF)
-    dhb[1] = pack2(dv).astype(BF)
     dcat = pack3(
         widen(pltpu.roll(dv, ROWS - 1, 0)), widen(dv), widen(pltpu.roll(dv, 1, 0))
     ).astype(BF)
@@ -561,6 +560,7 @@
     t3c = keep(r3_start(0))
     r1_finish(1, s1c)
     s2c = keep(r2_start(1))
+    dhb[1] = pack2(dv).astype(BF)
     dhalo = [
         send(dhb.at[1], dhb.at[0], dhs.at[0], dhr.at[0], row_peer(1)),
         send(dhb.at[1], dhb.at[2], dhs.at[1], dhr.at[1], row_peer(-1)),
@@ -571,11 +571,11 @@
     t4c = keep(g3_start(0))
     r2_finish(1, s2c)
     s3c = keep(r3_start(1))
+    g3_finish(0, t4c)
+    t5c = keep(g2_start(0))
     got(z2c)
     zy[pl.ds(i2, 1)] = in_order(zx)[None]
     z3c = keep(spread(zy, i2, 2, second_peer))
-    g3_finish(0, t4c)
-    t5c = keep(g2_start(0))
 
     got(dhalo)
 
@@ -591,10 +591,10 @@
 
     r3_finish(1, s3c)
     s4c = keep(g3_start(1))
+    got(t5c)
+    t6c = keep(g1_start(0))
     got(z3c)
     f_s[rest, pl.ds(zlane, 128)] = in_order(zy)
-    got(t5c)
-    t6c = keep(g1_start(0))
     g3_finish(1, s4c)
     s5c = keep(g2_start(1))
     z4c = keep(z4_start())

time: 75.5 us -> 75.6 us (level)
  no operation moved by 1% of the time
where the time goes in v5:
time: 75.6 us; the launch traced here: 75.5 us
  Pallas kernels  74.7 us (99%)
  between operations  0.8 us (1%)
    pallas_call x1, Pallas kernels, on_device(): pl.pallas_call(lambda *refs: mega(factor, *refs), out_shape=(jax.ShapeDty...  71.4 us
    pallas_call x1, Pallas kernels, on_device(): pl.pallas_call(lambda *refs: finish(factor, *refs), out_shape=(jax.ShapeD...  3.28 us

profile of v5, /device:TPU:1, one launch (start us, length us, event | category | flops | bytes accessed | tf_op | source)
XLA Modules:
  0.0 75.5 jit_solution(10833692814982882768)
XLA Ops:
  0.6 71.4 %mega.1 = (bf16[106,2,320]{2,1,0:T(2,128)(2,1)S(1)}, f32[3,320,320]{2,1,0:T(8,128)S(1)}, f32[320,960]{1,0:T(8,128)S(1)}, f32[320,320]{1,0:T(8,128)S(1)}, bf16[960,1024]{1,0:T(8,128)(2,1)S(1)}) custom-call(s32[16]{0:T(128)} %refs_0_.1, bf16[106,2,320]{2,1,0:T(2,128)(2,1)} %bitcast.9, bf16[106,2,320]{2,1,0:T(2,128)(2,1)} %bitcast.10, ...), custom_call_target="tpu_custom_call" | custom-call | tf_op jit(solution)/shard_map/mega/pallas_call | solution.py:664
  72.0 3.3 %finish.1 = (bf16[106,2,320]{2,1,0:T(2,128)(2,1)}, f32[3,3,320,320]{3,2,1,0:T(8,128)}, f32[3,320,320]{2,1,0:T(8,128)}, f32[320,960]{1,0:T(8,128)}, f32[320,320]{1,0:T(8,128)}) custom-call(bf16[106,2,320]{2,1,0:T(2,128)(2,1)S(1)} %get-tuple-element.15.refs_0_, f32[3,320,320]{2,1,0:T(8,128)S(1)} %get-tuple-element.16.refs_1_, ...), custom_call_target="tpu_custom_call" | custom-call | tf_op jit(solution)/shard_map/finish/pallas_call | solution.py:698

commit v6 on v4

--- a/solution.py
+++ b/solution.py
@@ -595,13 +595,13 @@
     f_s[rest, pl.ds(zlane, 128)] = in_order(zy)
     got(t5c)
     t6c = keep(g1_start(0))
+    t7c = g0_start(0, 0)
     g3_finish(1, s4c)
     s5c = keep(g2_start(1))
     z4c = keep(z4_start())
     got(s5c)
     s6c = keep(g1_start(1))
     s7c = g0_start(1, 0)
-    t7c = g0_start(0, 0)
     for cp, k in zip(t6c, NEAR_LAST[4]):
         cp.wait_recv()
         t7c += g0_start(0, k)

time: 75.5 us -> 75.5 us (level)
  no operation moved by 1% of the time
where the time goes in v6:
time: 75.5 us; the launch traced here: 75.4 us
  Pallas kernels  74.6 us (99%)
  between operations  0.8 us (1%)
    pallas_call x1, Pallas kernels, on_device(): pl.pallas_call(lambda *refs: mega(factor, *refs), out_shape=(jax.ShapeDty...  71.3 us
    pallas_call x1, Pallas kernels, on_device(): pl.pallas_call(lambda *refs: finish(factor, *refs), out_shape=(jax.ShapeD...  3.28 us

profile of v6, /device:TPU:1, one launch (start us, length us, event | category | flops | bytes accessed | tf_op | source)
XLA Modules:
  0.0 75.4 jit_solution(4467824754818552991)
XLA Ops:
  0.6 71.3 %mega.1 = (bf16[106,2,320]{2,1,0:T(2,128)(2,1)S(1)}, f32[3,320,320]{2,1,0:T(8,128)S(1)}, f32[320,960]{1,0:T(8,128)S(1)}, f32[320,320]{1,0:T(8,128)S(1)}, bf16[960,1024]{1,0:T(8,128)(2,1)S(1)}) custom-call(s32[16]{0:T(128)} %refs_0_.1, bf16[106,2,320]{2,1,0:T(2,128)(2,1)} %bitcast.9, bf16[106,2,320]{2,1,0:T(2,128)(2,1)} %bitcast.10, ...), custom_call_target="tpu_custom_call" | custom-call | tf_op jit(solution)/shard_map/mega/pallas_call | solution.py:664
  72.0 3.3 %finish.1 = (bf16[106,2,320]{2,1,0:T(2,128)(2,1)}, f32[3,3,320,320]{3,2,1,0:T(8,128)}, f32[3,320,320]{2,1,0:T(8,128)}, f32[320,960]{1,0:T(8,128)}, f32[320,320]{1,0:T(8,128)}) custom-call(bf16[106,2,320]{2,1,0:T(2,128)(2,1)S(1)} %get-tuple-element.15.refs_0_, f32[3,320,320]{2,1,0:T(8,128)S(1)} %get-tuple-element.16.refs_1_, ...), custom_call_target="tpu_custom_call" | custom-call | tf_op jit(solution)/shard_map/finish/pallas_call | solution.py:698
